TPU v7x, 128 devices: a whole 4x4x4 slice. The times are simulated.
128 devices in a mesh: ty: 16 (over x, y), tx: 8 (over z, core).
Axes of the slice: x: 4, y: 4, z: 4, core: 2. Of those that a mesh axis runs over, the one named last changes fastest.
Arguments:
- object_field: float32 [2, 12288, 4096], P(None, 'ty', 'tx'), may hold values from -6 to 6
- probe: float32 [2, 256, 256], replicated, may hold values from -6 to 6
- slot_counts: int32 [16, 8], P('ty', 'tx'), may hold values from 1 to 24, as said below
- positions: int32 [16, 8, 2, 24], P('ty', 'tx'), may hold values from 0 to 12032, as said below
- amplitude: float32 [16, 8, 24, 256, 256], P('ty', 'tx'), may hold values from 0.2 to 3
Outputs:
- new_object: float32 [2, 12288, 4096], P(None, 'ty', 'tx')
- new_probe: float32 [2, 256, 256], replicated
Inputs may be any that keep to these rules, and one draw needn't show every extreme that they name: Each tile has at least one live slot and some tile has exactly 24; slots at index slot_counts or above are unused. `positions`: A slot's corner lies inside the tile that holds the slot, and its 256 x 256 patch lies inside the object; the patch may reach into the tiles below and to the right.
All inputs are finite; a program needn't handle non-finite values.
Results may differ from a plain program's by a relative error of at most 0.0001.
Values sent between devices are 32-bit elements; how exact they have to be, the bound alone decides.
No kernel may reach another device: no remote copies, remote signals or barrier semaphores. Data moves between devices by JAX's collectives and lax.ppermute only.
A program may use at most 128 MiB of HBM per device.

v0:
```python
import math

import jax
import jax.numpy as jnp
from jax import lax
from jax.sharding import PartitionSpec as P


def passed_along(value, axis, steps):
    count = lax.axis_size(axis)
    leading, last = (max(0, -steps), min(count, count - steps))
    return lax.ppermute(value, axis, [(source, source + steps) for source in range(leading, last)])


def dft_tables(size):
    index = lax.iota(jnp.int32, size)
    product = index[:, None] * index[None, :] % size
    angle = product.astype(jnp.float32) * (2.0 * math.pi / size)
    scale = 1.0 / math.sqrt(size)
    real_part = jnp.cos(angle) * scale
    imag_part = -jnp.sin(angle) * scale
    first = jnp.concatenate(
        [jnp.concatenate([real_part, -imag_part], 1), jnp.concatenate([imag_part, real_part], 1)], 0
    )
    second = jnp.concatenate(
        [jnp.concatenate([real_part, imag_part], 1), jnp.concatenate([-imag_part, real_part], 1)], 0
    )
    return (first, second)


def transform(real_in, imag_in, left, right):
    size = real_in.shape[0]
    stacked = jnp.concatenate([real_in, imag_in], 0)
    middle = jnp.dot(
        left, stacked, precision=lax.Precision.HIGHEST, preferred_element_type=jnp.float32
    )
    beside = jnp.concatenate([middle[:size], middle[size:]], 1)
    result = jnp.dot(
        beside, right, precision=lax.Precision.HIGHEST, preferred_element_type=jnp.float32
    )
    return (result[:, :size], result[:, size:])


def correct(patch, probe, amp, tables):
    first, second = tables
    pr = probe[0]
    pi = probe[1]
    orr = patch[0]
    oi = patch[1]
    er = pr * orr - pi * oi
    ei = pr * oi + pi * orr
    fr, fi = transform(er, ei, first, second)
    scale = amp / jnp.sqrt(fr * fr + fi * fi + 0.25) - 1.0
    wr, wi = transform(fr * scale, fi * scale, second, first)
    grad = jnp.stack([pr * wr + pi * wi, pr * wi - pi * wr])
    numer = jnp.stack([orr * wr + oi * wi, orr * wi - oi * wr])
    return (grad, numer, orr * orr + oi * oi)


def add_patch(acc, update, row, col):
    zero = jnp.zeros((), jnp.int32)
    current = lax.dynamic_slice(acc, (zero, row, col), update.shape)
    return lax.dynamic_update_slice(acc, current + update, (zero, row, col))


def local(object_field, probe, slot_counts, positions, amplitude):
    size = probe.shape[1]
    tile_rows = object_field.shape[1]
    tile_cols = object_field.shape[2]
    tables = dft_tables(size)
    illum_patch = (probe[0] * probe[0] + probe[1] * probe[1])[None]
    base_row = lax.axis_index("ty") * tile_rows
    base_col = lax.axis_index("tx") * tile_cols
    rows = positions[0, 0, 0] - base_row
    cols = positions[0, 0, 1] - base_col
    amps = amplitude[0, 0]
    count = slot_counts[0, 0]
    zero = jnp.zeros((), jnp.int32)
    east = passed_along(object_field[:, :, :size], "tx", -1)
    wider = jnp.concatenate([object_field, east], 2)
    south = passed_along(wider[:, :size, :], "ty", -1)
    extended = jnp.concatenate([wider, south], 1)
    acc = jnp.zeros((3, tile_rows + size, tile_cols + size), jnp.float32)
    pnum = jnp.zeros((2, size, size), jnp.float32)
    pden = jnp.zeros((size, size), jnp.float32)

    def slot_work(source, slot, carry):
        acc_now, pnum_now, pden_now = carry
        row = rows[slot]
        col = cols[slot]
        patch = lax.dynamic_slice(source, (zero, row, col), (2, size, size))
        grad, numer, denom = correct(patch, probe, amps[slot], tables)
        acc_now = add_patch(acc_now, jnp.concatenate([grad, illum_patch], 0), row, col)
        return (acc_now, pnum_now + numer, pden_now + denom)

    def own_step(slot, carry):
        return slot_work(extended, slot, carry)

    acc, pnum, pden = lax.fori_loop(0, count, own_step, (acc, pnum, pden))
    below = passed_along(acc[:, tile_rows:, :], "ty", 1)
    acc = acc[:, :tile_rows, :]
    acc = jnp.concatenate([acc[:, :size, :] + below, acc[:, size:, :]], 1)
    right = passed_along(acc[:, :, tile_cols:], "tx", 1)
    acc = acc[:, :, :tile_cols]
    acc = jnp.concatenate([acc[:, :, :size] + right, acc[:, :, size:]], 2)
    new_object = object_field + acc[0:2] / (acc[2][None] + 1.0)
    pnum_all, pden_all = lax.psum((pnum, pden), ("ty", "tx"))
    new_probe = probe + pnum_all / (pden_all[None] + 1.0)
    return (new_object, new_probe)


def solution(mesh):
    in_specs = (
        P(None, "ty", "tx"),
        P(),
        P("ty", "tx"),
        P("ty", "tx", None, None),
        P("ty", "tx", None, None, None),
    )
    out_specs = (P(None, "ty", "tx"), P())
    return jax.shard_map(local, mesh=mesh, in_specs=in_specs, out_specs=out_specs, check_vma=False)
```

profile of v0, /device:TPU:1, one launch (start us, length us, event | category | flops | bytes accessed | tf_op | source)
XLA Modules:
  0.0 986.9 jit_solution(6589988333079946671)
XLA Ops:
  8.9 3.3 collective-permute-start
  12.6 19.7 %collective-permute-done = f32[2,768,256]{2,1,0:T(8,128)S(1)} collective-permute-done((f32[2,768,256]{2,1,0:T(8,128)S(1)}, f32[2,768,256]{2,1,0:T(8,128)S(1)}, u32[]{:S(2)}, u32[]{:S(2)}) %collective-permute-start) | collective-permute-done | bytes 1572896 | tf_op jit(solution)/shard_map/ppermute | solution.py:12
  32.4 2.1 copy-done.4
  40.1 17.7 %collective-permute-done.1 = f32[2,256,768]{2,1,0:T(8,128)} collective-permute-done((f32[2,256,768]{2,1,0:T(8,128)}, f32[2,256,768]{2,1,0:T(8,128)}, u32[]{:S(2)}, u32[]{:S(2)}) %collective-permute-start.1) | collective-permute-done | bytes 1572896 | tf_op jit(solution)/shard_map/ppermute | solution.py:12
  57.9 5.9 pad_maximum_fusion
  65.3 4.4 broadcast_in_dim.6
  69.7 322.0 %while.16 = (s32[]{:T(128)}, f32[3,1024,768]{2,1,0:T(8,128)}, f32[2,256,256]{2,1,0:T(8,128)}, f32[256,256]{1,0:T(8,128)}, s32[]{:T(128)}, /*index=5*/s32[24]{0:T...) while((s32[]{:T(128)}, f32[3,1024,768]{2,1,0:T(8,128)}, ...), condition=%wide.region_1.2_spmd, body=%wide.region_0.1_spmd.sunk | while | flops 3224567808 | bytes 23069060 | solution.py:99
  77.0 1.9 convolution_bitcast_fusion.4
  84.0 2.1 add_bitcast_fusion.2
  87.8 1.9 maximum_add_fusion.5
  89.7 9.6 dynamic_update_slice.7
  106.4 1.9 convolution_bitcast_fusion.4
  113.4 2.1 add_bitcast_fusion.2
  117.2 1.9 maximum_add_fusion.5
  119.1 9.0 dynamic_update_slice.7
  135.1 1.9 convolution_bitcast_fusion.4
  142.2 2.1 add_bitcast_fusion.2
  145.9 1.9 maximum_add_fusion.5
  147.8 9.3 dynamic_update_slice.7
  168.3 1.9 convolution_bitcast_fusion.5
  171.2 2.1 add_bitcast_fusion.2
  175.0 1.9 maximum_add_fusion.5
  176.9 9.6 dynamic_update_slice.7
  193.6 1.9 convolution_bitcast_fusion.4
  197.6 1.9 convolution_bitcast_fusion.5
  200.6 2.1 add_bitcast_fusion.2
  204.4 1.9 maximum_add_fusion.5
  206.3 9.6 dynamic_update_slice.7
  222.9 1.9 convolution_bitcast_fusion.4
  227.0 1.9 convolution_bitcast_fusion.5
  230.0 2.1 add_bitcast_fusion.2
  233.7 1.9 maximum_add_fusion.5
  235.6 9.2 dynamic_update_slice.7
  251.9 1.9 convolution_bitcast_fusion.4
  259.0 2.1 add_bitcast_fusion.2
  262.7 1.9 maximum_add_fusion.5
  264.6 9.6 dynamic_update_slice.7
  281.3 1.9 convolution_bitcast_fusion.4
  285.4 1.9 convolution_bitcast_fusion.5
  288.4 2.1 add_bitcast_fusion.2
  292.1 1.9 maximum_add_fusion.5
  294.0 9.6 dynamic_update_slice.7
  310.6 1.9 convolution_bitcast_fusion.4
  314.7 1.9 convolution_bitcast_fusion.5
  317.7 2.1 add_bitcast_fusion.2
  321.4 1.9 maximum_add_fusion.5
  323.4 9.2 dynamic_update_slice.7
  343.7 1.9 convolution_bitcast_fusion.5
  346.7 2.1 add_bitcast_fusion.2
  350.4 1.9 maximum_add_fusion.5
  352.3 9.5 dynamic_update_slice.7
  369.0 1.9 convolution_bitcast_fusion.4
  373.0 1.9 convolution_bitcast_fusion.5
  376.0 2.1 add_bitcast_fusion.2
  379.8 1.9 maximum_add_fusion.5
  381.7 9.4 dynamic_update_slice.7
  395.0 2.6 slice.130
  397.6 23.0 %collective-permute-done.2 = f32[3,256,768]{2,1,0:T(8,128)S(1)} collective-permute-done((f32[3,256,768]{2,1,0:T(8,128)S(1)}, f32[3,256,768]{2,1,0:T(8,128)S(1)}, u32[]{:S(2)}, u32[]{:S(2)}) %collective-permute-start.2) | collective-permute-done | bytes 2359328 | tf_op jit(solution)/shard_map/ppermute | solution.py:12
  420.6 2.0 slice_add_fusion
  424.1 1.9 collective-permute-start.3
  426.1 543.2 %all-reduce.3.cloned.1.call-done = (f32[2,256,256]{2,1,0:T(8,128)}, f32[256,256]{1,0:T(8,128)}) async-done(((f32[2,256,256]{2,1,0:T(8,128)}, f32[256,256]{1,0:T(8,128)}), (f32[2,256,256]{2,1,0:T(8,128)}, f32[256,256]{1,0:T(8,128)})) %all-reduce.3.cloned.1.call-update) | async-done | bytes 786448 | tf_op jit(solution)/shard_map/psum | solution.py:107
  970.2 2.1 divide_add_fusion
  972.3 2.5 fusion.31
  977.4 2.6 fusion.28
  (164 shorter events, 110.0 us)
Async XLA Ops:
  7.2 962.1 %all-reduce.3.cloned.1.call-start = ((), (), s32[]{:S(2)}) async-start(), calls=%async_computation | async-start | bytes 1572864 | tf_op jit(solution)/shard_map/psum | solution.py:107
  7.2 5.0 copy-start.2
  8.9 23.4 %collective-permute-start = (f32[2,768,256]{2,1,0:T(8,128)S(1)}, f32[2,768,256]{2,1,0:T(8,128)S(1)}, u32[]{:S(2)}, u32[]{:S(2)}) collective-permute-start(f32[2,768,256]{2,1,0:T(8,128)S(1)} %slice.124), channel_id=1, source_target_pairs={{1,0},{2,1},{3,2},{4,3},{5,4},{6,5},{7,6},{9,8},{10,9},{11,10},{12... | collective-permute-start | bytes 4718600 | tf_op jit(solution)/shard_map/ppermute | solution.py:12
  12.5 26.8 %copy-start.6 = (s32[1,1,2,24]{3,2,1,0:T(2,128)S(1)}, s32[1,1,2,24]{3,2,1,0:T(2,128)}, u32[]{:S(2)}) copy-start(s32[1,1,2,24]{3,2,1,0:T(2,128)} %param.10) | copy-start | bytes 580
  12.6 26.8 %copy-start = (f32[2,256,256]{2,1,0:T(8,128)S(1)}, f32[2,256,256]{2,1,0:T(8,128)}, u32[]{:S(2)}) copy-start(f32[2,256,256]{2,1,0:T(8,128)} %param.8) | copy-start | bytes 1572868
  32.4 2.1 copy-start.4
  35.8 22.1 %collective-permute-start.1 = (f32[2,256,768]{2,1,0:T(8,128)}, f32[2,256,768]{2,1,0:T(8,128)}, u32[]{:S(2)}, u32[]{:S(2)}) collective-permute-start(f32[2,256,768]{2,1,0:T(8,128)} %slice.144), channel_id=1, source_target_pairs={{8,0},{16,8},{24,16},{32,24},{40,32},{48,40},{56,48},{64,56},{72,6... | collective-permute-start | bytes 4718600 | tf_op jit(solution)/shard_map/ppermute | solution.py:12
  80.0 6.2 copy-start.5
  109.3 6.2 copy-start.5
  138.1 6.2 copy-start.5
  167.2 6.2 copy-start.5
  196.5 6.2 copy-start.5
  225.9 6.2 copy-start.5
  254.9 6.2 copy-start.5
  284.3 6.2 copy-start.5
  313.6 6.2 copy-start.5
  342.6 6.2 copy-start.5
  372.0 6.2 copy-start.5
  393.5 27.1 %collective-permute-start.2 = (f32[3,256,768]{2,1,0:T(8,128)S(1)}, f32[3,256,768]{2,1,0:T(8,128)S(1)}, u32[]{:S(2)}, u32[]{:S(2)}) collective-permute-start(f32[3,256,768]{2,1,0:T(8,128)S(1)} %slice.129), channel_id=1, source_target_pairs={{0,8},{8,16},{16,24},{24,32},{32,40},{40,48},{48,56},{56,64},{64,7... | collective-permute-start | bytes 7077896 | tf_op jit(solution)/shard_map/ppermute | solution.py:12
  397.6 26.5 %copy-start.1 = (f32[3,512,768]{2,1,0:T(8,128)}, f32[3,512,768]{2,1,0:T(8,128)S(1)}, u32[]{:S(2)}) copy-start(f32[3,512,768]{2,1,0:T(8,128)S(1)} %slice.130) | copy-start | bytes 14155780
  424.1 548.2 %collective-permute-start.3 = (f32[3,768,256]{2,1,0:T(8,128)}, f32[3,768,256]{2,1,0:T(8,128)}, u32[]{:S(2)}, u32[]{:S(2)}) collective-permute-start(f32[3,768,256]{2,1,0:T(8,128)} %fusion.29), channel_id=1, source_target_pairs={{0,1},{1,2},{2,3},{3,4},{4,5},{5,6},{6,7},{8,9},{9,10},{10,11},{11... | collective-permute-start | bytes 7077896 | tf_op jit(solution)/shard_map/ppermute | solution.py:12
  970.2 4.6 slice-start
  972.3 2.5 slice-start.1
  975.5 1.9 copy-start.3
Sparse Core Ops, SparseCore 0:
  426.2 542.9 all-reduce.2
where the time goes:
time: 997 us; the launch traced here: 987 us
  waiting for transfers between devices  604 us (61%)
  local copies, waits for them, and re-layouts  135 us (14%)
  other arithmetic  110 us (11%)
  matrix products  64.4 us (6%)
  loops' own time  51.7 us (5%)
  between operations  14.3 us (1%)
    psum x1, waiting for transfers between devices, local(): pnum_all, pden_all = lax.psum((pnum, pden), ('ty', 'tx'))  543 us
    dynamic_update_slice x11, local copies, waits for them, and re-layouts, add_patch(): return lax.dynamic_update_slice(acc, current + update, (zero, row, col))  103 us
    ppermute x4, waiting for transfers between devices, passed_along(): lax.ppermute(value, axis, [(source, source + steps) for source in range(l...  60.4 us
    another operation x1, loops' own time, local(): acc, pnum, pden = lax.fori_loop(0, count, own_step, (acc, pnum, pden))  51.7 us
    dot_general x22, matrix products, transform(): jnp.dot(left, stacked, precision=lax.Precision.HIGHEST, preferred_element...  41 us
    another operation x11, other arithmetic, correct(): numer = jnp.stack([orr * wr + oi * wi, orr * wi - oi * wr])  23.6 us
    dot_general x22, matrix products, transform(): jnp.dot(beside, right, precision=lax.Precision.HIGHEST, preferred_element...  23.3 us
    add x11, other arithmetic, slot_work(): return (acc_now, pnum_now + numer, pden_now + denom)  21 us
  transfers between devices with their start and end apart: 5, of which 4 were waited for; matrix products, arithmetic and copies ran while one was open for 1% of the time, Pallas kernels for 0%

commit v1 on v0

v1 whole, which is shorter than its diff:
```python
import functools

import jax
import jax.numpy as jnp
import ml_dtypes
import numpy as np
from jax import lax
from jax.experimental import pallas as pl
from jax.experimental.pallas import tpu as pltpu
from jax.sharding import PartitionSpec as P

SIZE = 256
HALF = 128
ROWS = 768
COLS = 512
CAP = 24
CH = 16
AXES = ("ty", "tx")
VMEM_LIMIT = 56 * 1024 * 1024


def halves(matrix):
    high = matrix.astype(ml_dtypes.bfloat16)
    low = (matrix - high.astype(np.float64)).astype(ml_dtypes.bfloat16)
    return high, low


def left_table(m):
    real = np.block([[m.real, -m.imag], [m.imag, m.real]])
    high, low = halves(real)
    return np.concatenate([high, high, low], 1)


def right_table(m):
    real = np.block([[m.real, m.imag], [-m.imag, m.real]])
    high, low = halves(real)
    return np.concatenate([high, high, low], 0)


@functools.lru_cache(maxsize=None)
def tables():
    n = np.arange(HALF)
    even = 2 * n
    odd_row = 2 * n + 1
    odd_col = 2 * ((n + HALF // 2) % HALF) + 1

    def dft(freq):
        turns = (freq[:, None] * n[None, :]) % SIZE
        return np.exp(-2j * np.pi * turns / SIZE) / np.sqrt(SIZE)

    left = np.stack(
        [
            left_table(dft(even)),
            left_table(dft(odd_row)),
            left_table(np.conj(dft(even)).T),
            left_table(np.conj(dft(odd_row)).T),
        ]
    )
    right = np.stack(
        [
            right_table(dft(even).T),
            right_table(dft(odd_col).T),
            right_table(np.conj(dft(even))),
            right_table(np.conj(dft(odd_col))),
        ]
    )
    return left, right


def split(x):
    high = x.astype(jnp.bfloat16)
    low = (x - high.astype(jnp.float32)).astype(jnp.bfloat16)
    return high, low


def dot(a, b):
    return jnp.dot(a, b, preferred_element_type=jnp.float32)


def lanes(rows):
    return lax.broadcasted_iota(jnp.int32, (rows, HALF), 1)


def corner_of(pos_ref, k):
    row = lax.rem(pos_ref[0, k], ROWS)
    col = lax.rem(pos_ref[1, k], COLS)
    return row, lax.div(col, HALF), lax.rem(col, HALF)


def rolled(a, b, s, low_first):
    ra = pltpu.roll(a, s, 1)
    rb = pltpu.roll(b, s, 1)
    return jnp.where(low_first, ra, rb), jnp.where(low_first, rb, ra)


def illum_kernel(count_ref, pos_ref, probe_ref, acc_ref, power):
    acc_ref[...] = jnp.zeros_like(acc_ref)
    for j in range(2):
        re = probe_ref[0, :, HALF * j : HALF * (j + 1)]
        im = probe_ref[1, :, HALF * j : HALF * (j + 1)]
        power[j] = re * re + im * im

    def body(k, carry):
        row, tile, s = corner_of(pos_ref, k)
        for i in range(0, SIZE, CH):
            ge = lanes(CH) >= s
            p0, p1 = rolled(power[0, i : i + CH], power[1, i : i + CH], s, ge)
            at = pl.ds(row + i, CH)
            acc_ref[tile, at, :] += jnp.where(ge, p0, 0.0)
            acc_ref[tile + 1, at, :] += p1
            acc_ref[tile + 2, at, :] += jnp.where(ge, 0.0, p0)
        return carry

    lax.fori_loop(0, count_ref[0, 0], body, 0)


def slots_kernel(
    count_ref, pos_ref, own_ref, east_ref, south_ref, corner_ref, amp_ref, probe_ref, left_ref, right_ref,
    acc_ref, sums_ref,
    ext, prob, patch, xs, ys, zs, fs, amp, piece_sem, amp_sem,
):
    count = count_ref[0, 0]

    def amp_copies(k, slot):
        return [
            pltpu.make_async_copy(amp_ref.at[k, :, pl.ds(HALF * j, HALF)], amp.at[slot, j], amp_sem.at[slot, j])
            for j in range(2)
        ]

    for copy in amp_copies(0, 0):
        copy.start()
    pieces = []
    for c in range(2):
        for t in range(6):
            for below in range(2):
                if t < 4:
                    source = (south_ref if below else own_ref).at[c, :, pl.ds(HALF * t, HALF)]
                else:
                    source = (corner_ref if below else east_ref).at[c, :, pl.ds(HALF * (t - 4), HALF)]
                target = ext.at[c, t, pl.ds(ROWS, SIZE) if below else pl.ds(0, ROWS)]
                pieces.append(pltpu.make_async_copy(source, target, piece_sem.at[len(pieces)]))
    for copy in pieces:
        copy.start()
    acc_ref[...] = jnp.zeros_like(acc_ref)
    sums_ref[...] = jnp.zeros_like(sums_ref)
    for copy in pieces:
        copy.wait()

    def body(k, carry):
        slot = lax.rem(k, 2)

        @pl.when(k + 1 < count)
        def _():
            for copy in amp_copies(k + 1, 1 - slot):
                copy.start()

        row, tile, s = corner_of(pos_ref, k)
        ge = lanes(CH) >= s
        for i in range(0, HALF, CH):
            waves = []
            for h in range(2):
                at = HALF * h + i
                span = slice(at, at + CH)
                pr = rolled(probe_ref[0, span, :HALF], probe_ref[0, span, HALF:], s, ge)
                pi = rolled(probe_ref[1, span, :HALF], probe_ref[1, span, HALF:], s, ge)
                where = pl.ds(row + at, CH)
                obj = []
                for c in range(2):
                    first = jnp.where(ge, ext[c, tile, where, :], ext[c, tile + 2, where, :])
                    obj.append((first, ext[c, tile + 1, where, :]))
                for j in range(2):
                    prob[0, j, span] = pr[j]
                    prob[1, j, span] = pi[j]
                    patch[0, j, span] = obj[0][j]
                    patch[1, j, span] = obj[1][j]
                waves.append(
                    [
                        (pr[j] * obj[0][j] - pi[j] * obj[1][j], pr[j] * obj[1][j] + pi[j] * obj[0][j])
                        for j in range(2)
                    ]
                )
            for j in range(2):
                col = slice(HALF * j, HALF * (j + 1))
                for c in range(2):
                    top, low = waves[0][j][c], waves[1][j][c]
                    for p, value in ((0, top + low), (1, top - low)):
                        hi, lo = split(value)
                        xs[p, HALF * c + i : HALF * c + i + CH, col] = hi
                        xs[p, SIZE + HALF * c + i : SIZE + HALF * c + i + CH, col] = lo

        def left_dot(table, p):
            ys[p] = dot(left_ref[table, :, : 2 * SIZE], xs[p]) + dot(left_ref[table, :, 2 * SIZE :], xs[p, :SIZE])

        def right_dot(table, p):
            fs[p] = dot(zs[p], right_ref[table, : 2 * SIZE]) + dot(zs[p, :, :SIZE], right_ref[table, 2 * SIZE :])

        def put_z(p, rows, c, value):
            hi, lo = split(value)
            zs[p, rows, HALF * c : HALF * (c + 1)] = hi
            zs[p, rows, SIZE + HALF * c : SIZE + HALF * (c + 1)] = lo

        left_dot(0, 0)
        left_dot(1, 1)
        for r in range(2):
            for i in range(0, HALF, CH):
                rows = slice(HALF * r + i, HALF * r + i + CH)
                for c in range(2):
                    span = slice(HALF * c + i, HALF * c + i + CH)
                    a, b = ys[r, span, :HALF], ys[r, span, HALF:]
                    put_z(0, rows, c, a + b)
                    put_z(1, rows, c, a - b)
        right_dot(0, 0)
        right_dot(1, 1)
        for copy in amp_copies(k, slot):
            copy.wait()
        lane = lanes(CH)
        near = lane < HALF // 2
        pick0 = jnp.where(near, 2 * lane, 2 * lane - (HALF - 1))
        pick1 = jnp.where(near, 2 * lane + 1, 2 * lane - HALF)
        for r in range(2):
            for i in range(0, HALF, CH):
                rows = slice(HALF * r + i, HALF * r + i + CH)
                a0 = amp[slot, 0, pl.ds(2 * i + r, CH, stride=2), :]
                a1 = amp[slot, 1, pl.ds(2 * i + r, CH, stride=2), :]
                v0 = jnp.take_along_axis(a0, pick0, axis=1)
                v1 = jnp.take_along_axis(a1, pick1, axis=1)
                for p, value in ((0, jnp.where(near, v0, v1)), (1, jnp.where(near, v1, v0))):
                    fr, fi = fs[p, rows, :HALF], fs[p, rows, HALF:]
                    scale = value * lax.rsqrt(fr * fr + fi * fi + 0.25) - 1.0
                    put_z(p, rows, 0, fr * scale)
                    put_z(p, rows, 1, fi * scale)
        right_dot(2, 0)
        right_dot(3, 1)
        for r in range(2):
            for i in range(0, HALF, CH):
                rows = slice(HALF * r + i, HALF * r + i + CH)
                for c in range(2):
                    lane_part = slice(HALF * c, HALF * (c + 1))
                    a, b = fs[0, rows, lane_part], fs[1, rows, lane_part]
                    for j, value in ((0, a + b), (1, a - b)):
                        hi, lo = split(value)
                        col = slice(HALF * j, HALF * (j + 1))
                        xs[r, HALF * c + i : HALF * c + i + CH, col] = hi
                        xs[r, SIZE + HALF * c + i : SIZE + HALF * c + i + CH, col] = lo
        left_dot(2, 0)
        left_dot(3, 1)
        back_shift = lax.rem(HALF - s, HALF)
        fit = lane < HALF - s
        for i in range(0, HALF, CH):
            for h in range(2):
                at = HALF * h + i
                span = slice(at, at + CH)
                grads = []
                numer = []
                denom = []
                for j in range(2):
                    col = slice(HALF * j, HALF * (j + 1))
                    w = []
                    for c in range(2):
                        part = slice(HALF * c + i, HALF * c + i + CH)
                        a, b = ys[0, part, col], ys[1, part, col]
                        w.append(a - b if h else a + b)
                    pr, pi = prob[0, j, span], prob[1, j, span]
                    orr, oi = patch[0, j, span], patch[1, j, span]
                    grads.append((pr * w[0] + pi * w[1], pr * w[1] - pi * w[0]))
                    numer.append((orr * w[0] + oi * w[1], orr * w[1] - oi * w[0]))
                    denom.append(orr * orr + oi * oi)
                where = pl.ds(row + at, CH)
                for c in range(2):
                    acc_ref[c, tile, where, :] += jnp.where(ge, grads[0][c], 0.0)
                    acc_ref[c, tile + 1, where, :] += grads[1][c]
                    acc_ref[c, tile + 2, where, :] += jnp.where(ge, 0.0, grads[0][c])
                    n0, n1 = rolled(numer[0][c], numer[1][c], back_shift, fit)
                    sums_ref[c, 0, span] += n0
                    sums_ref[c, 1, span] += n1
                d0, d1 = rolled(denom[0], denom[1], back_shift, fit)
                sums_ref[2, 0, span] += d0
                sums_ref[2, 1, span] += d1
        return carry

    lax.fori_loop(0, count, body, 0)


def final_kernel(own_ref, acc_ref, illum_ref, b_ref, bi_ref, r_ref, ri_ref, out_ref):
    for t in range(4):
        for i in range(0, ROWS, CH * 2):
            rows = slice(i, i + CH * 2)
            den = illum_ref[t, rows] + 1.0
            num = [acc_ref[0, t, rows], acc_ref[1, t, rows]]
            if i < SIZE:
                den += bi_ref[t, rows]
                num = [num[c] + b_ref[c, t, rows] for c in range(2)]
            if t < 2:
                den += ri_ref[t, rows]
                num = [num[c] + r_ref[c, t, rows] for c in range(2)]
            col = slice(HALF * t, HALF * (t + 1))
            for c in range(2):
                out_ref[c, rows, col] = own_ref[c, rows, col] + num[c] / den


def shift(value, axis, step):
    count = lax.axis_size(axis)
    pairs = [(i, i + step) for i in range(count) if 0 <= i + step < count]
    return lax.ppermute(value, axis, pairs)


def smem():
    return pl.BlockSpec(memory_space=pltpu.SMEM)


def vmem():
    return pl.BlockSpec(memory_space=pltpu.VMEM)


def anywhere():
    return pl.BlockSpec(memory_space=pl.ANY)


def params():
    return pltpu.CompilerParams(vmem_limit_bytes=VMEM_LIMIT)


def rims(acc):
    lead = acc.ndim - 3
    east = lax.slice_in_dim(acc, 4, 6, axis=lead)
    corner = shift(lax.slice_in_dim(east, ROWS, ROWS + SIZE, axis=lead + 1), "tx", 1)
    right = shift(lax.slice_in_dim(east, 0, ROWS, axis=lead + 1), "tx", 1)
    south = lax.slice_in_dim(lax.slice_in_dim(acc, 0, 4, axis=lead), ROWS, ROWS + SIZE, axis=lead + 1)
    pad = jnp.concatenate(
        [
            lax.slice_in_dim(south, 0, 2, axis=lead) + corner,
            lax.slice_in_dim(south, 2, 4, axis=lead),
        ],
        lead,
    )
    return shift(pad, "ty", 1), right


def reduced(value):
    devices = lax.axis_size(AXES)
    parts = value.reshape(devices, -1, HALF)
    mine = lax.all_to_all(parts, AXES, 0, 0, tiled=True).sum(0)
    shared = lax.all_to_all(jnp.broadcast_to(mine[None], parts.shape), AXES, 0, 0, tiled=True)
    return shared.reshape(value.shape)


def local(object_field, probe, slot_counts, positions, amplitude):
    f32 = jnp.float32
    pos = positions.reshape(2, CAP)
    amps = amplitude.reshape(CAP, SIZE, SIZE)
    left, right = (jnp.asarray(t) for t in tables())

    south = shift(object_field[:, :SIZE, :], "ty", -1)
    east = shift(object_field[:, :, :SIZE], "tx", -1)
    corner = shift(south[:, :, :SIZE], "tx", -1)

    illum = pl.pallas_call(
        illum_kernel,
        out_shape=jax.ShapeDtypeStruct((6, ROWS + SIZE, HALF), f32),
        in_specs=[smem(), smem(), vmem()],
        out_specs=vmem(),
        scratch_shapes=[pltpu.VMEM((2, SIZE, HALF), f32)],
        compiler_params=params(),
        name="illum",
    )(slot_counts, pos, probe)
    illum_below, illum_right = rims(illum)

    acc, sums = pl.pallas_call(
        slots_kernel,
        out_shape=(
            jax.ShapeDtypeStruct((2, 6, ROWS + SIZE, HALF), f32),
            jax.ShapeDtypeStruct((3, 2, SIZE, HALF), f32),
        ),
        in_specs=[smem(), smem()] + [anywhere()] * 5 + [vmem()] * 3,
        out_specs=(vmem(), vmem()),
        scratch_shapes=[
            pltpu.VMEM((2, 6, ROWS + SIZE, HALF), f32),
            pltpu.VMEM((2, 2, SIZE, HALF), f32),
            pltpu.VMEM((2, 2, SIZE, HALF), f32),
            pltpu.VMEM((2, 2 * SIZE, SIZE), jnp.bfloat16),
            pltpu.VMEM((2, SIZE, SIZE), f32),
            pltpu.VMEM((2, SIZE, 2 * SIZE), jnp.bfloat16),
            pltpu.VMEM((2, SIZE, SIZE), f32),
            pltpu.VMEM((2, 2, SIZE, HALF), f32),
            pltpu.SemaphoreType.DMA((24,)),
            pltpu.SemaphoreType.DMA((2, 2)),
        ],
        compiler_params=params(),
        name="slots",
    )(slot_counts, pos, object_field, east, south, corner, amps, probe, left, right)

    below, beside = rims(acc)
    sums = reduced(sums.reshape(3 * 2 * SIZE, HALF)).reshape(3, 2, SIZE, HALF)
    new_object = pl.pallas_call(
        final_kernel,
        out_shape=jax.ShapeDtypeStruct((2, ROWS, COLS), f32),
        in_specs=[vmem()] * 7,
        out_specs=vmem(),
        compiler_params=params(),
        name="final",
    )(object_field, acc, illum, below, illum_below, beside, illum_right)
    sums = jnp.concatenate([sums[:, 0], sums[:, 1]], 2)
    new_probe = probe + sums[:2] / (sums[2][None] + 1.0)
    return (new_object, new_probe)


def solution(mesh):
    in_specs = (
        P(None, "ty", "tx"),
        P(),
        P("ty", "tx"),
        P("ty", "tx", None, None),
        P("ty", "tx", None, None, None),
    )
    out_specs = (P(None, "ty", "tx"), P())
    return jax.shard_map(local, mesh=mesh, in_specs=in_specs, out_specs=out_specs, check_vma=False)
```

time: 997 us -> 199 us (0.20)
  waiting for transfers between devices: 604 us -> 56.3 us
  local copies, waits for them, and re-layouts: 135 us -> 16 us
  other arithmetic: 110 us -> 5.35 us
  Pallas kernels: 0 us -> 65.1 us
  matrix products: 64.4 us -> 0 us
  loops' own time: 51.7 us -> 0 us
  starting transfers between devices: 8 us -> 50.8 us
  between operations: 14.3 us -> 1.44 us
    psum x1 -> x0, waiting for transfers between devices: 543 us -> none  [local(): pnum_all, pden_all = lax.psum((pnum, pden), ('ty', 'tx'))]
    dynamic_update_slice x11 -> x0, local copies, waits for them, and re-layouts: 103 us -> none  [add_patch(): return lax.dynamic_update_slice(acc, current + update, (zero, row, col))]
    pallas_call x0 -> x3, Pallas kernels: none -> 65.1 us  [the longest x1 51.4 us: local(): pl.pallas_call(slots_kernel, out_shape=(jax.ShapeDtypeStruct((2, 6, ROWS...]
    dot_general x44 -> x0, matrix products: 64.4 us -> none  [the longest x22 41 us: transform(): jnp.dot(left, stacked, precision=lax.Precision.HIGHEST, preferred_element...]
    another operation x1 -> x0, loops' own time: 51.7 us -> none  [local(): acc, pnum, pden = lax.fori_loop(0, count, own_step, (acc, pnum, pden))]
    add x28 -> x3, other arithmetic: 49.3 us -> 3.31 us  [the longest x2 2.45 us: rims(): lax.slice_in_dim(south, 0, 2, axis=lead) + corner]
    all_to_all x0 -> x2, starting transfers between devices: none -> 24.8 us  [the longest x1 15.8 us: reduced(): mine = lax.all_to_all(parts, AXES, 0, 0, tiled=True).sum(0)]
    another operation x11 -> x0, other arithmetic: 23.6 us -> none  [correct(): numer = jnp.stack([orr * wr + oi * wi, orr * wi - oi * wr])]
  transfers between devices with their start and end apart: 5 -> 11, of which waited for: 4 -> 5; matrix products, arithmetic and copies ran while one was open for 1% -> 8% of each run, Pallas kernels for 0% -> 3%
where the time goes in v1:
time: 199 us; the launch traced here: 195 us
  Pallas kernels  65.1 us (33%)
  waiting for transfers between devices  56.3 us (28%)
  starting transfers between devices  50.8 us (26%)
  local copies, waits for them, and re-layouts  16 us (8%)
  other arithmetic  5.35 us (3%)
    ppermute x9, waiting for transfers between devices, shift(): return lax.ppermute(value, axis, pairs)  56.2 us
    pallas_call x1, Pallas kernels, local(): pl.pallas_call(slots_kernel, out_shape=(jax.ShapeDtypeStruct((2, 6, ROWS...  51.4 us
    ppermute x9, starting transfers between devices, shift(): return lax.ppermute(value, axis, pairs)  26 us
    all_to_all x1, starting transfers between devices, reduced(): mine = lax.all_to_all(parts, AXES, 0, 0, tiled=True).sum(0)  15.8 us
    all_to_all x1, starting transfers between devices, reduced(): lax.all_to_all(jnp.broadcast_to(mine[None], parts.shape), AXES, 0, 0, til...  9.03 us
    pallas_call x1, Pallas kernels, local(): pl.pallas_call(final_kernel, out_shape=jax.ShapeDtypeStruct((2, ROWS, COL...  8 us
    pallas_call x1, Pallas kernels, local(): pl.pallas_call(illum_kernel, out_shape=jax.ShapeDtypeStruct((6, ROWS + SI...  5.77 us
    slice x2, local copies, waits for them, and re-layouts, rims(): right = shift(lax.slice_in_dim(east, 0, ROWS, axis=lead + 1), 'tx', 1)  4.73 us
  transfers between devices with their start and end apart: 11, of which 5 were waited for; matrix products, arithmetic and copies ran while one was open for 8% of the time, Pallas kernels for 3%

profile of v1, /device:TPU:1, one launch (start us, length us, event | category | flops | bytes accessed | tf_op | source)
XLA Modules:
  0.0 195.1 jit_solution(9272557642147119500)
XLA Ops:
  0.6 1.3 slice.62
  1.9 1.3 collective-permute-start.1
  3.2 1.5 slice.61
  4.7 3.3 %collective-permute-start = (f32[2,768,256]{2,1,0:T(8,128)S(1)}, f32[2,768,256]{2,1,0:T(8,128)S(1)}, u32[]{:S(2)}, u32[]{:S(2)}) collective-permute-start(f32[2,768,256]{2,1,0:T(8,128)S(1)} %slice.61), channel_id=1, source_target_pairs={{1,0},{2,1},{3,2},{4,3},{5,4},{6,5},{7,6},{9,8},{10,9},{11,10},{12... | collective-permute-start | bytes 4718600 | tf_op jit(solution)/shard_map/ppermute | solution.py:304
  8.1 20.4 %collective-permute-done.1.south_ref = f32[2,256,512]{2,1,0:T(8,128)S(1)} collective-permute-done((f32[2,256,512]{2,1,0:T(8,128)S(1)}, f32[2,256,512]{2,1,0:T(8,128)S(1)}, u32[]{:S(2)}, u32[]{:S(2)}) %collective-permute-start.1) | collective-permute-done | bytes 1048608 | tf_op jit(solution)/shard_map/ppermute | solution.py:304
  28.4 0.0 copy-start.1
  28.5 3.5 %collective-permute-start.2 = (f32[2,256,256]{2,1,0:T(8,128)S(1)}, f32[2,256,256]{2,1,0:T(8,128)S(1)}, u32[]{:S(2)}, u32[]{:S(2)}) collective-permute-start(f32[2,256,256]{2,1,0:T(8,128)S(1)} %slice.76), channel_id=1, source_target_pairs={{1,0},{2,1},{3,2},{4,3},{5,4},{6,5},{7,6},{9,8},{10,9},{11,10},{12... | collective-permute-start | bytes 1572872 | tf_op jit(solution)/shard_map/ppermute | solution.py:304
  32.7 7.9 %collective-permute-done.2.corner_ref = f32[2,256,256]{2,1,0:T(8,128)S(1)} collective-permute-done((f32[2,256,256]{2,1,0:T(8,128)S(1)}, f32[2,256,256]{2,1,0:T(8,128)S(1)}, u32[]{:S(2)}, u32[]{:S(2)}) %collective-permute-start.2) | collective-permute-done | bytes 524320 | tf_op jit(solution)/shard_map/ppermute | solution.py:304
  40.6 0.0 copy-start.4
  40.6 0.0 collective-permute-done.east_ref
  40.6 0.0 copy-start.2
  40.6 0.0 copy-done.1
  40.6 0.8 copy-done.4
  41.4 0.5 copy-done.2
  41.9 51.4 %slots.1 = (f32[2,6,1024,128]{3,2,1,0:T(8,128)}, f32[3,2,256,128]{3,2,1,0:T(8,128)}) custom-call(s32[1,1]{1,0:T(1,128)S(6)} %copy.11.count_ref, s32[2,24]{1,0:T(2,128)} %bitcast.13, f32[2,768,512]{2,1,0:T(8,128)} %own_ref.3, f32[2,768,256]{2,1,0:T(8,128)} %copy-done.2, f32[2,256,512]{2,1,0:T(8,128)} %copy-done.1, f32[2,256,256]{2,1,0:T(8,128)} %copy-done.4, ...), custom_call_target="tpu_custom_call" | custom-call | tf_op jit(solution)/shard_map/slots/pallas_call | solution.py:368
  93.3 2.2 %reshape_reshape.6 = f32[128,12,128]{2,1,0:T(8,128)} reshape(f32[3,2,256,128]{3,2,1,0:T(8,128)} %get-tuple-element.5) | data formatting | bytes 1572864 | tf_op jit(solution)/shard_map/reshape;reshape | solution.py:341
  95.4 15.8 %all-to-all-start = ((f32[128,12,128]{2,1,0:T(8,128)}), f32[128,12,128]{2,1,0:T(8,128)S(1)}, u32[]{:S(2)}, u32[]{:S(2)}) async-start(f32[128,12,128]{2,1,0:T(8,128)} %reshape_reshape.6), calls=%async_computation | async-start | bytes 2097152 | tf_op jit(solution)/shard_map/all_to_all | solution.py:342
  111.2 1.1 slice.65
  112.3 3.7 %collective-permute-start.3 = (f32[2,2,256,128]{3,2,1,0:T(8,128)S(1)}, f32[2,2,256,128]{3,2,1,0:T(8,128)S(1)}, u32[]{:S(2)}, u32[]{:S(2)}) collective-permute-start(f32[2,2,256,128]{3,2,1,0:T(8,128)S(1)} %slice.65), channel_id=1, source_target_pairs={{0,1},{1,2},{2,3},{3,4},{4,5},{5,6},{6,7},{8,9},{9,10},{10,11},{11... | collective-permute-start | bytes 1572872 | tf_op jit(solution)/shard_map/ppermute | solution.py:304
  116.0 2.7 %slice.70 = f32[2,2,768,128]{3,2,1,0:T(8,128)} slice(f32[2,6,1024,128]{3,2,1,0:T(8,128)} %get-tuple-element.4.acc_ref), slice={[0:2], [4:6], [0:768], [0:128]} | slice | bytes 3145728 | tf_op jit(solution)/shard_map/slice | solution.py:327
  118.7 2.0 %collective-permute-start.7 = (f32[2,2,768,128]{3,2,1,0:T(8,128)}, f32[2,2,768,128]{3,2,1,0:T(8,128)}, u32[]{:S(2)}, u32[]{:S(2)}) collective-permute-start(f32[2,2,768,128]{3,2,1,0:T(8,128)} %slice.70), channel_id=1, source_target_pairs={{0,1},{1,2},{2,3},{3,4},{4,5},{5,6},{6,7},{8,9},{9,10},{10,11},{11... | collective-permute-start | bytes 4718600 | tf_op jit(solution)/shard_map/ppermute | solution.py:304
  120.7 5.8 %illum.1.illum_ref = f32[6,1024,128]{2,1,0:T(8,128)} custom-call(s32[1,1]{1,0:T(1,128)S(6)} %copy.11.count_ref, s32[2,24]{1,0:T(2,128)} %bitcast.14, f32[2,256,256]{2,1,0:T(8,128)} %probe_ref.3), custom_call_target="tpu_custom_call" | custom-call | tf_op jit(solution)/shard_map/illum/pallas_call | solution.py:357
  126.5 1.7 slice.78
  128.2 2.3 %collective-permute-start.5 = (f32[2,256,128]{2,1,0:T(8,128)}, f32[2,256,128]{2,1,0:T(8,128)}, u32[]{:S(2)}, u32[]{:S(2)}) collective-permute-start(f32[2,256,128]{2,1,0:T(8,128)} %slice.78), channel_id=1, source_target_pairs={{0,1},{1,2},{2,3},{3,4},{4,5},{5,6},{6,7},{8,9},{9,10},{10,11},{11... | collective-permute-start | bytes 786440 | tf_op jit(solution)/shard_map/ppermute | solution.py:304
  130.4 0.1 all-to-all-done
  130.5 0.1 reduce_sum.9
  130.7 1.1 broadcast_in_dim.2
  131.8 9.0 %all-to-all-start.1 = ((f32[128,12,128]{2,1,0:T(8,128)}), f32[128,12,128]{2,1,0:T(8,128)S(1)}, u32[]{:S(2)}, u32[]{:S(2)}) async-start(f32[128,12,128]{2,1,0:T(8,128)} %broadcast_in_dim.2), calls=%async_computation.1 | async-start | bytes 2097152 | tf_op jit(solution)/shard_map/all_to_all | solution.py:343
  140.8 0.0 collective-permute-done.3
  140.8 1.3 slice_add_fusion
  142.1 1.0 pad_maximum_fusion
  143.1 3.3 %collective-permute-start.4 = (f32[2,4,256,128]{3,2,1,0:T(8,128)}, f32[2,4,256,128]{3,2,1,0:T(8,128)S(1)}, u32[]{:S(2)}, u32[]{:S(2)}) collective-permute-start(f32[2,4,256,128]{3,2,1,0:T(8,128)} %pad_maximum_fusion), channel_id=1, source_target_pairs={{0,8},{8,16},{16,24},{24,32},{32,40},{40,48},{48,56},{56,64},{64,7... | collective-permute-start | bytes 3145736 | tf_op jit(solution)/shard_map/ppermute | solution.py:304
  146.5 2.1 %slice.80 = f32[2,768,128]{2,1,0:T(8,128)} slice(f32[6,1024,128]{2,1,0:T(8,128)} %illum.1.illum_ref), slice={[4:6], [0:768], [0:128]} | slice | bytes 1572864 | tf_op jit(solution)/shard_map/slice | solution.py:327
  148.6 0.0 copy-start
  148.6 3.9 %collective-permute-start.8 = (f32[2,768,128]{2,1,0:T(8,128)}, f32[2,768,128]{2,1,0:T(8,128)}, u32[]{:S(2)}, u32[]{:S(2)}) collective-permute-start(f32[2,768,128]{2,1,0:T(8,128)} %slice.80), channel_id=1, source_target_pairs={{0,1},{1,2},{2,3},{3,4},{4,5},{5,6},{6,7},{8,9},{9,10},{10,11},{11... | collective-permute-start | bytes 2359304 | tf_op jit(solution)/shard_map/ppermute | solution.py:304
  152.5 8.0 %collective-permute-done.5 = f32[2,256,128]{2,1,0:T(8,128)} collective-permute-done((f32[2,256,128]{2,1,0:T(8,128)}, f32[2,256,128]{2,1,0:T(8,128)}, u32[]{:S(2)}, u32[]{:S(2)}) %collective-permute-start.5) | collective-permute-done | bytes 262176 | tf_op jit(solution)/shard_map/ppermute | solution.py:304
  160.5 1.2 slice_add_fusion.1
  161.7 0.8 pad_maximum_fusion.1
  162.6 2.6 %collective-permute-start.6 = (f32[4,256,128]{2,1,0:T(8,128)}, f32[4,256,128]{2,1,0:T(8,128)}, u32[]{:S(2)}, u32[]{:S(2)}) collective-permute-start(f32[4,256,128]{2,1,0:T(8,128)} %pad_maximum_fusion.1), channel_id=1, source_target_pairs={{0,8},{8,16},{16,24},{24,32},{32,40},{40,48},{48,56},{56,64},{64,7... | collective-permute-start | bytes 1572872 | tf_op jit(solution)/shard_map/ppermute | solution.py:304
  165.1 0.0 all-to-all-done.1
  165.1 0.1 reshape_reshape.7
  165.2 0.1 slice_bitcast_fusion
  165.3 0.0 copy-done
  165.3 0.9 fusion.2
  166.2 20.0 %collective-permute-done.6.bi_ref = f32[4,256,128]{2,1,0:T(8,128)} collective-permute-done((f32[4,256,128]{2,1,0:T(8,128)}, f32[4,256,128]{2,1,0:T(8,128)}, u32[]{:S(2)}, u32[]{:S(2)}) %collective-permute-start.6) | collective-permute-done | bytes 524320 | tf_op jit(solution)/shard_map/ppermute | solution.py:304
  186.1 0.0 collective-permute-done.8.ri_ref
  186.1 0.0 collective-permute-done.4.b_ref
  186.1 0.0 copy-start.3
  186.1 0.0 collective-permute-done.7.r_ref
  186.1 0.9 copy-done.3
  187.1 8.0 %final.1 = f32[2,768,512]{2,1,0:T(8,128)} custom-call(f32[2,768,512]{2,1,0:T(8,128)} %own_ref.3, f32[2,6,1024,128]{3,2,1,0:T(8,128)} %get-tuple-element.4.acc_ref, f32[6,1024,128]{2,1,0:T(8,128)} %illum.1.illum_ref, f32[2,4,256,128]{3,2,1,0:T(8,128)} %copy-done.3, f32[4,256,128]{2,1,0:T(8,128)} %collective-permute-done.6.bi_ref, ...), custom_call_target="tpu_custom_call" | custom-call | tf_op jit(solution)/shard_map/final/pallas_call | solution.py:394
  (2 shorter events, 0.1 us)
Async XLA Ops:
  1.9 26.5 %collective-permute-start.1 = (f32[2,256,512]{2,1,0:T(8,128)S(1)}, f32[2,256,512]{2,1,0:T(8,128)S(1)}, u32[]{:S(2)}, u32[]{:S(2)}) collective-permute-start(f32[2,256,512]{2,1,0:T(8,128)S(1)} %slice.62), channel_id=1, source_target_pairs={{8,0},{16,8},{24,16},{32,24},{40,32},{48,40},{56,48},{64,56},{72,6... | collective-permute-start | bytes 3145736 | tf_op jit(solution)/shard_map/ppermute | solution.py:304
  4.7 35.8 %collective-permute-start = (f32[2,768,256]{2,1,0:T(8,128)S(1)}, f32[2,768,256]{2,1,0:T(8,128)S(1)}, u32[]{:S(2)}, u32[]{:S(2)}) collective-permute-start(f32[2,768,256]{2,1,0:T(8,128)S(1)} %slice.61), channel_id=1, source_target_pairs={{1,0},{2,1},{3,2},{4,3},{5,4},{6,5},{7,6},{9,8},{10,9},{11,10},{12... | collective-permute-start | bytes 4718600 | tf_op jit(solution)/shard_map/ppermute | solution.py:304
  28.4 12.1 %copy-start.1 = (f32[2,256,512]{2,1,0:T(8,128)}, f32[2,256,512]{2,1,0:T(8,128)S(1)}, u32[]{:S(2)}) copy-start(f32[2,256,512]{2,1,0:T(8,128)S(1)} %collective-permute-done.1.south_ref) | copy-start | bytes 3145732
  28.5 12.1 %collective-permute-start.2 = (f32[2,256,256]{2,1,0:T(8,128)S(1)}, f32[2,256,256]{2,1,0:T(8,128)S(1)}, u32[]{:S(2)}, u32[]{:S(2)}) collective-permute-start(f32[2,256,256]{2,1,0:T(8,128)S(1)} %slice.76), channel_id=1, source_target_pairs={{1,0},{2,1},{3,2},{4,3},{5,4},{6,5},{7,6},{9,8},{10,9},{11,10},{12... | collective-permute-start | bytes 1572872 | tf_op jit(solution)/shard_map/ppermute | solution.py:304
  40.6 0.8 copy-start.4
  40.6 1.3 copy-start.2
  95.4 35.1 %all-to-all-start = ((f32[128,12,128]{2,1,0:T(8,128)}), f32[128,12,128]{2,1,0:T(8,128)S(1)}, u32[]{:S(2)}, u32[]{:S(2)}) async-start(f32[128,12,128]{2,1,0:T(8,128)} %reshape_reshape.6), calls=%async_computation | async-start | bytes 2097152 | tf_op jit(solution)/shard_map/all_to_all | solution.py:342
  112.3 28.5 %collective-permute-start.3 = (f32[2,2,256,128]{3,2,1,0:T(8,128)S(1)}, f32[2,2,256,128]{3,2,1,0:T(8,128)S(1)}, u32[]{:S(2)}, u32[]{:S(2)}) collective-permute-start(f32[2,2,256,128]{3,2,1,0:T(8,128)S(1)} %slice.65), channel_id=1, source_target_pairs={{0,1},{1,2},{2,3},{3,4},{4,5},{5,6},{6,7},{8,9},{9,10},{10,11},{11... | collective-permute-start | bytes 1572872 | tf_op jit(solution)/shard_map/ppermute | solution.py:304
  118.7 67.5 %collective-permute-start.7 = (f32[2,2,768,128]{3,2,1,0:T(8,128)}, f32[2,2,768,128]{3,2,1,0:T(8,128)}, u32[]{:S(2)}, u32[]{:S(2)}) collective-permute-start(f32[2,2,768,128]{3,2,1,0:T(8,128)} %slice.70), channel_id=1, source_target_pairs={{0,1},{1,2},{2,3},{3,4},{4,5},{5,6},{6,7},{8,9},{9,10},{10,11},{11... | collective-permute-start | bytes 4718600 | tf_op jit(solution)/shard_map/ppermute | solution.py:304
  128.2 32.4 %collective-permute-start.5 = (f32[2,256,128]{2,1,0:T(8,128)}, f32[2,256,128]{2,1,0:T(8,128)}, u32[]{:S(2)}, u32[]{:S(2)}) collective-permute-start(f32[2,256,128]{2,1,0:T(8,128)} %slice.78), channel_id=1, source_target_pairs={{0,1},{1,2},{2,3},{3,4},{4,5},{5,6},{6,7},{8,9},{9,10},{10,11},{11... | collective-permute-start | bytes 786440 | tf_op jit(solution)/shard_map/ppermute | solution.py:304
  131.8 33.4 %all-to-all-start.1 = ((f32[128,12,128]{2,1,0:T(8,128)}), f32[128,12,128]{2,1,0:T(8,128)S(1)}, u32[]{:S(2)}, u32[]{:S(2)}) async-start(f32[128,12,128]{2,1,0:T(8,128)} %broadcast_in_dim.2), calls=%async_computation.1 | async-start | bytes 2097152 | tf_op jit(solution)/shard_map/all_to_all | solution.py:343
  143.1 43.0 %collective-permute-start.4 = (f32[2,4,256,128]{3,2,1,0:T(8,128)}, f32[2,4,256,128]{3,2,1,0:T(8,128)S(1)}, u32[]{:S(2)}, u32[]{:S(2)}) collective-permute-start(f32[2,4,256,128]{3,2,1,0:T(8,128)} %pad_maximum_fusion), channel_id=1, source_target_pairs={{0,8},{8,16},{16,24},{24,32},{32,40},{40,48},{48,56},{56,64},{64,7... | collective-permute-start | bytes 3145736 | tf_op jit(solution)/shard_map/ppermute | solution.py:304
  148.6 16.7 %copy-start = (f32[2,256,256]{2,1,0:T(8,128)S(1)}, f32[2,256,256]{2,1,0:T(8,128)}, u32[]{:S(2)}) copy-start(f32[2,256,256]{2,1,0:T(8,128)} %probe_ref.3) | copy-start | bytes 1572868
  148.6 37.6 %collective-permute-start.8 = (f32[2,768,128]{2,1,0:T(8,128)}, f32[2,768,128]{2,1,0:T(8,128)}, u32[]{:S(2)}, u32[]{:S(2)}) collective-permute-start(f32[2,768,128]{2,1,0:T(8,128)} %slice.80), channel_id=1, source_target_pairs={{0,1},{1,2},{2,3},{3,4},{4,5},{5,6},{6,7},{8,9},{9,10},{10,11},{11... | collective-permute-start | bytes 2359304 | tf_op jit(solution)/shard_map/ppermute | solution.py:304
  162.6 23.6 %collective-permute-start.6 = (f32[4,256,128]{2,1,0:T(8,128)}, f32[4,256,128]{2,1,0:T(8,128)}, u32[]{:S(2)}, u32[]{:S(2)}) collective-permute-start(f32[4,256,128]{2,1,0:T(8,128)} %pad_maximum_fusion.1), channel_id=1, source_target_pairs={{0,8},{8,16},{16,24},{24,32},{32,40},{40,48},{48,56},{56,64},{64,7... | collective-permute-start | bytes 1572872 | tf_op jit(solution)/shard_map/ppermute | solution.py:304
  186.1 1.0 copy-start.3

commit v2 on v0

v2 whole, which is shorter than its diff:
```python
import functools

import jax
import jax.numpy as jnp
import ml_dtypes
import numpy as np
from jax import lax
from jax.experimental import pallas as pl
from jax.experimental.pallas import tpu as pltpu
from jax.sharding import PartitionSpec as P

SIZE = 256
HALF = 128
ROWS = 768
COLS = 512
CAP = 24
CH = 16
SPARE = ROWS + SIZE
DEEP = SPARE + SIZE
AXES = ("ty", "tx")
VMEM_LIMIT = 48 * 1024 * 1024


def halves(matrix):
    high = matrix.astype(ml_dtypes.bfloat16)
    low = (matrix - high.astype(np.float64)).astype(ml_dtypes.bfloat16)
    return high, low


def left_table(m):
    real = np.block([[m.real, -m.imag], [m.imag, m.real]])
    high, low = halves(real)
    return np.concatenate([high, high, low], 1)


def right_table(m):
    real = np.block([[m.real, m.imag], [-m.imag, m.real]])
    high, low = halves(real)
    return np.concatenate([high, high, low], 0)


@functools.lru_cache(maxsize=None)
def tables():
    n = np.arange(HALF)
    even = 2 * n
    odd_row = 2 * n + 1
    odd_col = 2 * ((n + HALF // 2) % HALF) + 1

    def dft(freq):
        turns = (freq[:, None] * n[None, :]) % SIZE
        return np.exp(-2j * np.pi * turns / SIZE) / np.sqrt(SIZE)

    left = np.stack(
        [
            left_table(dft(even)),
            left_table(dft(odd_row)),
            left_table(np.conj(dft(even)).T),
            left_table(np.conj(dft(odd_row)).T),
        ]
    )
    right = np.stack(
        [
            right_table(dft(even).T),
            right_table(dft(odd_col).T),
            right_table(np.conj(dft(even))),
            right_table(np.conj(dft(odd_col))),
        ]
    )
    return left, right


def split(x):
    high = x.astype(jnp.bfloat16)
    low = (x - high.astype(jnp.float32)).astype(jnp.bfloat16)
    return high, low


def dot(a, b):
    return jnp.dot(a, b, preferred_element_type=jnp.float32)


def lanes(rows):
    return lax.broadcasted_iota(jnp.int32, (rows, HALF), 1)


def rolled(a, b, s, low_first):
    ra = pltpu.roll(a, s, 1)
    rb = pltpu.roll(b, s, 1)
    return jnp.where(low_first, ra, rb), jnp.where(low_first, rb, ra)


def slots_kernel(inside, *refs):
    if inside:
        count_ref, pos_ref, own_ref, amp_ref, probe_ref, left_ref, right_ref = refs[:7]
        own_out, sums_out = refs[7:9]
        refs = refs[9:]
    else:
        count_ref, pos_ref, own_ref, east_ref, south_ref, corner_ref, own_in, sums_in = refs[:8]
        amp_ref, probe_ref, left_ref, right_ref = refs[8:12]
        own_out, east_out, south_out, corner_out, parts_out = refs[12:17]
        refs = refs[17:]
    todo, ext, acc, sums, work_a, work_b, amp, piece_sem, acc_sem, amp_sem = refs

    pieces = []

    def piece(source, c, t, rows):
        pieces.append(pltpu.make_async_copy(source, ext.at[c, t, rows], piece_sem.at[len(pieces)]))

    for c in range(2):
        for t in range(6):
            span = pl.ds(HALF * (t % 4), HALF)
            if t < 4:
                piece(own_ref.at[c, :, span], c, t, pl.ds(0, ROWS))
            elif not inside:
                piece(east_ref.at[c, :, span], c, t, pl.ds(0, ROWS))
            if not inside:
                piece((south_ref if t < 4 else corner_ref).at[c, :, span], c, t, pl.ds(ROWS, SIZE))
    for copy in pieces:
        copy.start()
    earlier = []
    if not inside:
        earlier = [
            pltpu.make_async_copy(own_in, acc.at[:, pl.ds(0, 4), pl.ds(0, ROWS)], acc_sem.at[0]),
            pltpu.make_async_copy(sums_in, sums.at[0], acc_sem.at[1]),
        ]
    for copy in earlier:
        copy.start()

    def choose(k, found):
        row = lax.rem(pos_ref[0, k], ROWS)
        col = lax.rem(pos_ref[1, k], COLS)
        within = jnp.where(row <= ROWS - SIZE, 1, 0) * jnp.where(col <= COLS - SIZE, 1, 0)
        todo[0, found] = k
        todo[1, found] = row
        todo[2, found] = col
        return found + (within if inside else 1 - within)

    count = lax.fori_loop(0, count_ref[0, 0], choose, 0)
    todo[0, count] = 0
    todo[1, count] = SPARE
    todo[2, count] = 0
    pairs = lax.div(count + 1, 2)

    def amp_copies(k, slot):
        return [
            pltpu.make_async_copy(amp_ref.at[k, :, pl.ds(HALF * j, HALF)], amp.at[slot, j], amp_sem.at[slot, j])
            for j in range(2)
        ]

    def fetch(n, half):
        @pl.when(n < pairs)
        def _():
            for u in range(2):
                for copy in amp_copies(todo[0, 2 * n + u], half + u):
                    copy.start()

    fetch(0, 0)
    if inside:
        acc[:, :4, :ROWS] = jnp.zeros((3, 4, ROWS, HALF), jnp.float32)
        sums[0] = jnp.zeros((3, 2, SIZE, HALF), jnp.float32)
    else:
        acc[:, 4:, :SPARE] = jnp.zeros((3, 2, SPARE, HALF), jnp.float32)
        acc[:, :4, ROWS:SPARE] = jnp.zeros((3, 4, SIZE, HALF), jnp.float32)
    for copy in pieces + earlier:
        copy.wait()
    lane = lanes(CH)
    near = lane < HALF // 2
    pick0 = jnp.where(near, 2 * lane, 2 * lane - (HALF - 1))
    pick1 = jnp.where(near, 2 * lane + 1, 2 * lane - HALF)

    def stages(n, slot, work):
        xs, ys, zs, fs, prob, patch = work
        k = todo[0, n]
        row, col = todo[1, n], todo[2, n]
        tile, s = lax.div(col, HALF), lax.rem(col, HALF)
        kept = lax.div(row, SPARE)
        ge = lane >= s
        back_shift = lax.rem(HALF - s, HALF)
        fit = lane < HALF - s

        def put_x(p, i, c, j, value):
            hi, lo = split(value)
            col = slice(HALF * j, HALF * (j + 1))
            xs[p, pl.ds(HALF * c + i, CH), col] = hi
            xs[p, pl.ds(SIZE + HALF * c + i, CH), col] = lo

        def put_z(p, rows, c, value):
            hi, lo = split(value)
            zs[p, rows, HALF * c : HALF * (c + 1)] = hi
            zs[p, rows, SIZE + HALF * c : SIZE + HALF * (c + 1)] = lo

        def left_dot(table, p):
            ys[p] = dot(left_ref[table, :, : 2 * SIZE], xs[p]) + dot(left_ref[table, :, 2 * SIZE :], xs[p, :SIZE])

        def right_dot(table, p):
            fs[p] = dot(zs[p], right_ref[table, : 2 * SIZE]) + dot(zs[p, :, :SIZE], right_ref[table, 2 * SIZE :])

        def exit_wave(i):
            waves = []
            for h in range(2):
                span = pl.ds(HALF * h + i, CH)
                pr = rolled(probe_ref[0, span, :HALF], probe_ref[0, span, HALF:], s, ge)
                pi = rolled(probe_ref[1, span, :HALF], probe_ref[1, span, HALF:], s, ge)
                where = pl.ds(row + HALF * h + i, CH)
                obj = []
                for c in range(2):
                    first = jnp.where(ge, ext[c, tile, where, :], ext[c, tile + 2, where, :])
                    obj.append((first, ext[c, tile + 1, where, :]))
                for j in range(2):
                    prob[0, j, span] = pr[j]
                    prob[1, j, span] = pi[j]
                    patch[0, j, span] = obj[0][j]
                    patch[1, j, span] = obj[1][j]
                waves.append(
                    [
                        (pr[j] * obj[0][j] - pi[j] * obj[1][j], pr[j] * obj[1][j] + pi[j] * obj[0][j])
                        for j in range(2)
                    ]
                )
            for j in range(2):
                for c in range(2):
                    top, low = waves[0][j][c], waves[1][j][c]
                    put_x(0, i, c, j, top + low)
                    put_x(1, i, c, j, top - low)

        def column_split(i):
            for r in range(2):
                rows = pl.ds(HALF * r + i, CH)
                for c in range(2):
                    span = pl.ds(HALF * c + i, CH)
                    a, b = ys[r, span, :HALF], ys[r, span, HALF:]
                    put_z(0, rows, c, a + b)
                    put_z(1, rows, c, a - b)

        def correct(i):
            for r in range(2):
                rows = pl.ds(HALF * r + i, CH)
                a0 = amp[slot, 0, pl.ds(2 * i + r, CH, stride=2), :]
                a1 = amp[slot, 1, pl.ds(2 * i + r, CH, stride=2), :]
                v0 = jnp.take_along_axis(a0, pick0, axis=1)
                v1 = jnp.take_along_axis(a1, pick1, axis=1)
                for p, value in ((0, jnp.where(near, v0, v1)), (1, jnp.where(near, v1, v0))):
                    fr, fi = fs[p, rows, :HALF], fs[p, rows, HALF:]
                    scale = value * lax.rsqrt(fr * fr + fi * fi + 0.25) - 1.0
                    put_z(p, rows, 0, fr * scale)
                    put_z(p, rows, 1, fi * scale)

        def column_join(i):
            for r in range(2):
                rows = pl.ds(HALF * r + i, CH)
                for c in range(2):
                    part = slice(HALF * c, HALF * (c + 1))
                    a, b = fs[0, rows, part], fs[1, rows, part]
                    put_x(r, i, c, 0, a + b)
                    put_x(r, i, c, 1, a - b)

        def collect(i):
            w = {}
            for j in range(2):
                col = slice(HALF * j, HALF * (j + 1))
                for c in range(2):
                    part = pl.ds(HALF * c + i, CH)
                    a, b = ys[0, part, col], ys[1, part, col]
                    w[0, j, c] = a + b
                    w[1, j, c] = a - b
            for h in range(2):
                span = pl.ds(HALF * h + i, CH)
                grads = []
                numer = []
                denom = []
                for j in range(2):
                    wr, wi = w[h, j, 0], w[h, j, 1]
                    pr, pi = prob[0, j, span], prob[1, j, span]
                    orr, oi = patch[0, j, span], patch[1, j, span]
                    grads.append((pr * wr + pi * wi, pr * wi - pi * wr, pr * pr + pi * pi))
                    numer.append((orr * wr + oi * wi, orr * wi - oi * wr, orr * orr + oi * oi))
                where = pl.ds(row + HALF * h + i, CH)
                new = []
                for c in range(3):
                    new.append(acc[c, tile, where, :] + jnp.where(ge, grads[0][c], 0.0))
                    new.append(acc[c, tile + 1, where, :] + grads[1][c])
                    new.append(acc[c, tile + 2, where, :] + jnp.where(ge, 0.0, grads[0][c]))
                for c in range(3):
                    for t in range(3):
                        acc[c, tile + t, where, :] = new[3 * c + t]
                for c in range(3):
                    n0, n1 = rolled(numer[0][c], numer[1][c], back_shift, fit)
                    sums[kept, c, 0, span] += n0
                    sums[kept, c, 1, span] += n1

        def wait():
            for copy in amp_copies(k, slot):
                copy.wait()

        starts = range(0, HALF, CH)
        pair = lambda d, t: [functools.partial(d, t, 0), functools.partial(d, t + 1, 1)]
        each = lambda f: [functools.partial(f, i) for i in starts]
        return [
            each(exit_wave),
            pair(left_dot, 0),
            each(column_split),
            pair(right_dot, 0),
            [wait] + each(correct),
            pair(right_dot, 2),
            each(column_join),
            pair(left_dot, 2),
            each(collect),
        ]

    def body(n, carry):
        half = 2 * lax.rem(n, 2)
        fetch(n + 1, 2 - half)
        first = stages(2 * n, half, work_a)
        second = stages(2 * n + 1, half + 1, work_b)
        for m in range(len(first) + 1):
            for part in (second[m - 1] if m else []) + (first[m] if m < len(first) else []):
                part()
        return carry

    lax.fori_loop(0, pairs, body, 0)
    outs = [pltpu.make_async_copy(acc.at[:, pl.ds(0, 4), pl.ds(0, ROWS)], own_out, acc_sem.at[0])]
    if inside:
        outs.append(pltpu.make_async_copy(sums.at[0], sums_out, acc_sem.at[1]))
    else:
        south, east = pl.ds(ROWS, SIZE), pl.ds(4, 2)
        outs.append(pltpu.make_async_copy(acc.at[:, east, pl.ds(0, ROWS)], east_out, acc_sem.at[1]))
        outs.append(pltpu.make_async_copy(acc.at[:, pl.ds(0, 4), south], south_out, acc_sem.at[2]))
        outs.append(pltpu.make_async_copy(acc.at[:, east, south], corner_out, acc_sem.at[3]))
    for copy in outs:
        copy.start()
    if not inside:
        for j in range(2):

            def arrange(b, carry):
                for c in range(3):
                    rows = sums[0, c, j, pl.ds(pl.multiple_of(8 * b, 8), 8)]
                    for h in range(2):
                        parts_out[64 * j + 2 * b + h, 4 * c : 4 * c + 4] = rows[4 * h : 4 * h + 4]
                return carry

            lax.fori_loop(0, SIZE // 8, arrange, 0)
    for copy in outs:
        copy.wait()


def final_kernel(own_ref, acc_ref, right_ref, below_ref, corner_ref, out_ref):
    tile = pl.program_id(0)
    block = pl.program_id(1)

    def put(num):
        den = num[2] + 1.0
        for c in range(2):
            out_ref[c] = own_ref[c] + num[c] / den

    for near in (True, False):
        for top in (True, False):

            @pl.when(((tile < 2) == near) & ((block == 0) == top))
            def _():
                num = [acc_ref[c, 0] for c in range(3)]
                if near:
                    num = [num[c] + right_ref[c, 0] for c in range(3)]
                if top:
                    num = [num[c] + below_ref[c, 0] for c in range(3)]
                if near and top:
                    num = [num[c] + corner_ref[c, 0] for c in range(3)]
                put(num)


def shift(value, down, along):
    rows, cols = (lax.axis_size(axis) for axis in AXES)
    pairs = [
        (i * cols + j, (i + down) * cols + j + along)
        for i in range(rows)
        for j in range(cols)
        if 0 <= i + down < rows and 0 <= j + along < cols
    ]
    return lax.ppermute(value, AXES, pairs)


def smem():
    return pl.BlockSpec(memory_space=pltpu.SMEM)


def vmem():
    return pl.BlockSpec(memory_space=pltpu.VMEM)


def anywhere():
    return pl.BlockSpec(memory_space=pl.ANY)


def floats(*shape):
    return jax.ShapeDtypeStruct(shape, jnp.float32)


def run_slots(inside, inputs):
    own = floats(3, 4, ROWS, HALF)
    if inside:
        out_shape = (own, floats(3, 2, SIZE, HALF))
        out_specs = (anywhere(), anywhere())
    else:
        out_shape = (
            own,
            floats(3, 2, ROWS, HALF),
            floats(3, 4, SIZE, HALF),
            floats(3, 2, SIZE, HALF),
            floats(128, 12, HALF),
        )
        out_specs = (anywhere(),) * 4 + (vmem(),)
    work = [
        pltpu.VMEM((2, 2 * SIZE, SIZE), jnp.bfloat16),
        pltpu.VMEM((2, SIZE, SIZE), jnp.float32),
        pltpu.VMEM((2, SIZE, 2 * SIZE), jnp.bfloat16),
        pltpu.VMEM((2, SIZE, SIZE), jnp.float32),
        pltpu.VMEM((2, 2, SIZE, HALF), jnp.float32),
        pltpu.VMEM((2, 2, SIZE, HALF), jnp.float32),
    ]
    slots = CAP // 3 if inside else CAP * 2 // 3
    return pl.pallas_call(
        functools.partial(slots_kernel, inside),
        out_shape=out_shape,
        in_specs=[smem()] * 2 + [anywhere()] * (len(inputs) - 5) + [vmem()] * 3,
        out_specs=out_specs,
        scratch_shapes=[
            pltpu.SMEM((3, 32), jnp.int32),
            pltpu.VMEM((2, 6, DEEP, HALF), jnp.float32),
            pltpu.VMEM((3, 6, DEEP, HALF), jnp.float32),
            pltpu.VMEM((2, 3, 2, SIZE, HALF), jnp.float32),
            work,
            work,
            pltpu.VMEM((4, 2, SIZE, HALF), jnp.float32),
            pltpu.SemaphoreType.DMA((24,)),
            pltpu.SemaphoreType.DMA((4,)),
            pltpu.SemaphoreType.DMA((4, 2)),
        ],
        compiler_params=pltpu.CompilerParams(vmem_limit_bytes=VMEM_LIMIT),
        cost_estimate=pl.CostEstimate(
            flops=slots * 48 * SIZE**3, bytes_accessed=slots * SIZE * SIZE * 4, transcendentals=slots * SIZE * SIZE
        ),
        name="slots_inside" if inside else "slots_other",
    )(*inputs)


def finish(object_field, acc, right, below, corner):
    def right_at(t, i):
        return 0, jnp.minimum(t, 1), jnp.where(t < 2, i, 2), 0

    return pl.pallas_call(
        final_kernel,
        grid=(4, 3),
        out_shape=floats(2, ROWS, COLS),
        in_specs=[
            pl.BlockSpec((2, SIZE, HALF), lambda t, i: (0, i, t)),
            pl.BlockSpec((3, 1, SIZE, HALF), lambda t, i: (0, t, i, 0)),
            pl.BlockSpec((3, 1, SIZE, HALF), right_at),
            pl.BlockSpec((3, 1, SIZE, HALF), lambda t, i: (0, t, 0, 0)),
            pl.BlockSpec((3, 1, SIZE, HALF), lambda t, i: (0, jnp.minimum(t, 1), 0, 0)),
        ],
        out_specs=pl.BlockSpec((2, SIZE, HALF), lambda t, i: (0, i, t)),
        name="final",
    )(object_field, acc, right, below, corner)


def local(object_field, probe, slot_counts, positions, amplitude):
    pos = positions.reshape(2, CAP)
    amps = amplitude.reshape(CAP, SIZE, SIZE)
    left, right = (jnp.asarray(t) for t in tables())
    south = shift(object_field[:, :SIZE, :], -1, 0)
    east = shift(object_field[:, :, :SIZE], 0, -1)
    corner = shift(object_field[:, :SIZE, :SIZE], -1, -1)
    common = (amps, probe, left, right)
    own_part, sums = run_slots(True, (slot_counts, pos, object_field) + common)
    acc, to_right, to_below, to_corner, parts = run_slots(
        False, (slot_counts, pos, object_field, east, south, corner, own_part, sums) + common
    )
    mine = lax.all_to_all(parts, AXES, 0, 0, tiled=True).sum(0).reshape(3, 4, HALF)
    new_object = finish(object_field, acc, shift(to_right, 0, 1), shift(to_below, 1, 0), shift(to_corner, 1, 1))
    me = lax.axis_index(AXES)
    held = lax.dynamic_slice(probe, (0, lax.rem(me, 64) * 4, lax.div(me, 64) * HALF), (2, 4, HALF))
    fresh = (held + mine[:2] / (mine[2][None] + 1.0)).reshape(1, 8, HALF)
    shared = lax.all_to_all(jnp.broadcast_to(fresh, (128, 8, HALF)), AXES, 0, 0, tiled=True)
    new_probe = shared.reshape(2, 64, 2, 4, HALF).transpose(2, 1, 3, 0, 4).reshape(2, SIZE, SIZE)
    return (new_object, new_probe)


def solution(mesh):
    in_specs = (
        P(None, "ty", "tx"),
        P(),
        P("ty", "tx"),
        P("ty", "tx", None, None),
        P("ty", "tx", None, None, None),
    )
    out_specs = (P(None, "ty", "tx"), P())
    return jax.shard_map(local, mesh=mesh, in_specs=in_specs, out_specs=out_specs, check_vma=False)
```

time: 997 us -> 190 us (0.19)
  waiting for transfers between devices: 604 us -> 45.2 us
  local copies, waits for them, and re-layouts: 135 us -> 7.94 us
  other arithmetic: 110 us -> 0.23 us
  matrix products: 64.4 us -> 0 us
  blocking collectives: 0 us -> 54 us
  loops' own time: 51.7 us -> 0 us
  starting transfers between devices: 8 us -> 50.6 us
  Pallas kernels: 0 us -> 28.7 us
  between operations: 14.3 us -> 1.46 us
    psum x1 -> x0, waiting for transfers between devices: 543 us -> none  [local(): pnum_all, pden_all = lax.psum((pnum, pden), ('ty', 'tx'))]
    dynamic_update_slice x11 -> x0, local copies, waits for them, and re-layouts: 103 us -> none  [add_patch(): return lax.dynamic_update_slice(acc, current + update, (zero, row, col))]
    dot_general x44 -> x0, matrix products: 64.4 us -> none  [the longest x22 41 us: transform(): jnp.dot(left, stacked, precision=lax.Precision.HIGHEST, preferred_element...]
    all_to_all x0 -> x1, blocking collectives: none -> 54 us  [local(): lax.all_to_all(jnp.broadcast_to(fresh, (128, 8, HALF)), AXES, 0, 0, tiled...]
    another operation x1 -> x0, loops' own time: 51.7 us -> none  [local(): acc, pnum, pden = lax.fori_loop(0, count, own_step, (acc, pnum, pden))]
    add x28 -> x2, other arithmetic: 49.3 us -> 0.09 us  [local(): fresh = (held + mine[:2] / (mine[2][None] + 1.0)).reshape(1, 8, HALF)]
    ppermute x4 -> x6, waiting for transfers between devices: 60.4 us -> 30.1 us  [shift(): return lax.ppermute(value, AXES, pairs)]
    pallas_call x0 -> x3, Pallas kernels: none -> 28.7 us  [the longest x2 18.7 us: run_slots(): pl.pallas_call(functools.partial(slots_kernel, inside), out_shape=out_sha...]
  transfers between devices with their start and end apart: 5 -> 7, of which waited for: 4 -> 2; matrix products, arithmetic and copies ran while one was open for 1% -> 2% of each run, Pallas kernels for 0% -> 3%
where the time goes in v2:
time: 190 us; the launch traced here: 188 us
  blocking collectives  54 us (28%)
  starting transfers between devices  50.6 us (27%)
  waiting for transfers between devices  45.2 us (24%)
  Pallas kernels  28.7 us (15%)
  local copies, waits for them, and re-layouts  7.94 us (4%)
    all_to_all x1, blocking collectives, local(): lax.all_to_all(jnp.broadcast_to(fresh, (128, 8, HALF)), AXES, 0, 0, tiled...  54 us
    ppermute x6, waiting for transfers between devices, shift(): return lax.ppermute(value, AXES, pairs)  30.1 us
    ppermute x6, starting transfers between devices, shift(): return lax.ppermute(value, AXES, pairs)  29.8 us
    all_to_all x1, starting transfers between devices, local(): lax.all_to_all(parts, AXES, 0, 0, tiled=True).sum(0).reshape(3, 4, HALF)  20.8 us
    pallas_call x2, Pallas kernels, run_slots(): pl.pallas_call(functools.partial(slots_kernel, inside), out_shape=out_sha...  18.7 us
    all_to_all x1, waiting for transfers between devices, local(): lax.all_to_all(parts, AXES, 0, 0, tiled=True).sum(0).reshape(3, 4, HALF)  15.1 us
    pallas_call x1, Pallas kernels, finish(): pl.pallas_call(final_kernel, grid=(4, 3), out_shape=floats(2, ROWS, COLS)...  10 us
  transfers between devices with their start and end apart: 7, of which 2 were waited for; matrix products, arithmetic and copies ran while one was open for 2% of the time, Pallas kernels for 3%

profile of v2, /device:TPU:1, one launch (start us, length us, event | category | flops | bytes accessed | tf_op | source)
XLA Modules:
  0.0 188.1 jit_solution(17150100700075923839)
XLA Ops:
  0.6 0.0 copy-start.3
  0.6 1.6 slice.19
  2.3 0.0 copy-start
  2.3 0.0 copy-start.1
  2.3 0.0 copy-start.2
  2.3 3.5 %collective-permute-start = (f32[2,768,256]{2,1,0:T(8,128)S(1)}, f32[2,768,256]{2,1,0:T(8,128)S(1)}, u32[]{:S(2)}, u32[]{:S(2)}) collective-permute-start(f32[2,768,256]{2,1,0:T(8,128)S(1)} %slice.19), channel_id=1, source_target_pairs={{1,0},{2,1},{3,2},{4,3},{5,4},{6,5},{7,6},{9,8},{10,9},{11,10},{12... | collective-permute-start | bytes 4718600 | tf_op jit(solution)/shard_map/ppermute | solution.py:378
  5.8 1.3 slice.20
  7.1 1.3 collective-permute-start.1
  8.4 1.1 slice.21
  9.5 1.3 collective-permute-start.2
  11.4 0.0 copy-done.3
  11.4 0.0 copy-done
  11.4 0.0 copy-done.1
  11.5 0.0 copy-done.2
  11.5 4.9 %slots_inside.1 = (f32[3,4,768,128]{3,2,1,0:T(8,128)}, f32[3,2,256,128]{3,2,1,0:T(8,128)S(1)}) custom-call(s32[1,1]{1,0:T(1,128)S(6)} %copy.12.refs_0_, s32[2,24]{1,0:T(2,128)S(1)} %bitcast.7, f32[2,768,512]{2,1,0:T(8,128)} %own_ref.1, f32[24,256,256]{2,1,0:T(8,128)} %bitcast.12, f32[2,256,256]{2,1,0:T(8,128)S(1)} %copy-done, ...), custom_call_target="tpu_custom_call" | custom-call | flops 6442450944 | bytes 2097152 | tf_op jit(solution)/shard_map/slots_inside/pallas_call | solution.py:420
  16.4 30.1 %collective-permute-done.2.refs_5_ = f32[2,256,256]{2,1,0:T(8,128)S(1)} collective-permute-done((f32[2,256,256]{2,1,0:T(8,128)S(1)}, f32[2,256,256]{2,1,0:T(8,128)S(1)}, u32[]{:S(2)}, u32[]{:S(2)}) %collective-permute-start.2) | collective-permute-done | bytes 524320 | tf_op jit(solution)/shard_map/ppermute | solution.py:378
  46.5 0.0 collective-permute-done.1.refs_4_
  46.5 0.0 collective-permute-done.refs_3_
  46.5 0.0 copy-start.5
  46.5 1.2 copy-done.5
  47.7 13.8 %slots_other.1 = (f32[3,4,768,128]{3,2,1,0:T(8,128)}, f32[3,2,768,128]{3,2,1,0:T(8,128)}, f32[3,4,256,128]{3,2,1,0:T(8,128)}, f32[3,2,256,128]{3,2,1,0:T(8,128)S(1)}, f32[128,12,128]{2,1,0:T(8,128)}) custom-call(s32[1,1]{1,0:T(1,128)S(6)} %copy.12.refs_0_, s32[2,24]{1,0:T(2,128)S(1)} %bitcast.8, f32[2,768,512]{2,1,0:T(8,128)} %own_ref.1, ...), custom_call_target="tpu_custom_call" | custom-call | flops 12884901888 | bytes 4194304 | tf_op jit(solution)/shard_map/slots_other/pallas_call | solution.py:420
  61.5 15.6 %collective-permute-start.3 = (f32[3,2,768,128]{3,2,1,0:T(8,128)}, f32[3,2,768,128]{3,2,1,0:T(8,128)}, u32[]{:S(2)}, u32[]{:S(2)}) collective-permute-start(f32[3,2,768,128]{3,2,1,0:T(8,128)} %get-tuple-element.12), channel_id=1, source_target_pairs={{0,1},{1,2},{2,3},{3,4},{4,5},{5,6},{6,7},{8,9},{9,10},{10,11},{11... | collective-permute-start | bytes 7077896 | tf_op jit(solution)/shard_map/ppermute | solution.py:378
  77.1 20.8 %all-to-all-start = ((f32[128,12,128]{2,1,0:T(8,128)}), f32[128,12,128]{2,1,0:T(8,128)S(1)}, u32[]{:S(2)}, u32[]{:S(2)}) async-start(f32[128,12,128]{2,1,0:T(8,128)} %get-tuple-element.15), calls=%async_computation | async-start | bytes 2097152 | tf_op jit(solution)/shard_map/all_to_all | solution.py:477
  97.9 4.5 %collective-permute-start.4 = (f32[3,4,256,128]{3,2,1,0:T(8,128)}, f32[3,4,256,128]{3,2,1,0:T(8,128)}, u32[]{:S(2)}, u32[]{:S(2)}) collective-permute-start(f32[3,4,256,128]{3,2,1,0:T(8,128)} %get-tuple-element.13), channel_id=1, source_target_pairs={{0,8},{1,9},{2,10},{3,11},{4,12},{5,13},{6,14},{7,15},{8,16},{9,17... | collective-permute-start | bytes 4718600 | tf_op jit(solution)/shard_map/ppermute | solution.py:378
  102.5 3.6 %collective-permute-start.5 = (f32[3,2,256,128]{3,2,1,0:T(8,128)S(1)}, f32[3,2,256,128]{3,2,1,0:T(8,128)S(1)}, u32[]{:S(2)}, u32[]{:S(2)}) collective-permute-start(f32[3,2,256,128]{3,2,1,0:T(8,128)S(1)} %get-tuple-element.14), channel_id=1, source_target_pairs={{0,9},{1,10},{2,11},{3,12},{4,13},{5,14},{6,15},{8,17},{9,18},{10,... | collective-permute-start | bytes 2359304 | tf_op jit(solution)/shard_map/ppermute | solution.py:378
  106.1 15.1 %all-to-all-done = f32[128,12,128]{2,1,0:T(8,128)S(1)} async-done(((f32[128,12,128]{2,1,0:T(8,128)}), f32[128,12,128]{2,1,0:T(8,128)S(1)}, u32[]{:S(2)}, u32[]{:S(2)}) %all-to-all-start) | async-done | bytes 786464 | tf_op jit(solution)/shard_map/all_to_all | solution.py:477
  121.1 0.1 reduce_sum.9
  121.3 0.1 divide_add_fusion
  121.4 54.0 %all_to_all.10 = f32[128,8,128]{2,1,0:T(8,128)S(1)} all-to-all(f32[128,8,128]{2,1,0:T(8,128)S(1)} %broadcast_in_dim.8), channel_id=1, replica_groups=mesh['ty'=16,'tx'=8] {'ty','tx'}, dimensions={0} | all-to-all | bytes 1048576 | tf_op jit(solution)/shard_map/all_to_all | solution.py:482
  175.4 0.1 copy.10
  175.5 0.4 copy.11
  175.9 1.2 reshape.26
  177.2 0.0 collective-permute-done.5.corner_ref
  177.2 0.0 copy-start.4
  177.2 0.0 collective-permute-done.4.below_ref
  177.2 0.0 collective-permute-done.3.right_ref
  177.2 1.0 copy-done.4
  178.1 10.0 %final.1 = f32[2,768,512]{2,1,0:T(8,128)} custom-call(f32[2,768,512]{2,1,0:T(8,128)} %own_ref.1, f32[3,4,768,128]{3,2,1,0:T(8,128)} %get-tuple-element.11.acc_ref, f32[3,2,768,128]{3,2,1,0:T(8,128)} %collective-permute-done.3.right_ref, f32[3,4,256,128]{3,2,1,0:T(8,128)} %collective-permute-done.4.below_ref, f32[3,2,256,128]{3,2,1,0:T(8,128)} %copy-done.4), custom_call_target="tpu_custom_call" | custom-call | tf_op jit(solution)/shard_map/final/pallas_call | solution.py:449
  (3 shorter events, 0.0 us)
Async XLA Ops:
  0.6 10.8 %copy-start.3 = (bf16[4,768,256]{2,1,0:T(8,128)(2,1)S(1)}, bf16[4,768,256]{2,1,0:T(8,128)(2,1)}, u32[]{:S(2)}) copy-start(bf16[4,768,256]{2,1,0:T(8,128)(2,1)} %constant.35.clone.refs_6_.refs_11_) | copy-start | bytes 4718596
  2.3 9.2 %copy-start = (f32[2,256,256]{2,1,0:T(8,128)S(1)}, f32[2,256,256]{2,1,0:T(8,128)}, u32[]{:S(2)}) copy-start(f32[2,256,256]{2,1,0:T(8,128)} %refs_9_.1) | copy-start | bytes 1572868
  2.3 9.2 %copy-start.1 = (s32[1,1,2,24]{3,2,1,0:T(2,128)S(1)}, s32[1,1,2,24]{3,2,1,0:T(2,128)}, u32[]{:S(2)}) copy-start(s32[1,1,2,24]{3,2,1,0:T(2,128)} %param.10) | copy-start | bytes 580
  2.3 9.2 %copy-start.2 = (bf16[4,256,768]{2,1,0:T(8,128)(2,1)S(1)}, bf16[4,256,768]{2,1,0:T(8,128)(2,1)}, u32[]{:S(2)}) copy-start(bf16[4,256,768]{2,1,0:T(8,128)(2,1)} %constant.34.clone.refs_5_.refs_10_) | copy-start | bytes 4718596
  2.3 44.2 %collective-permute-start = (f32[2,768,256]{2,1,0:T(8,128)S(1)}, f32[2,768,256]{2,1,0:T(8,128)S(1)}, u32[]{:S(2)}, u32[]{:S(2)}) collective-permute-start(f32[2,768,256]{2,1,0:T(8,128)S(1)} %slice.19), channel_id=1, source_target_pairs={{1,0},{2,1},{3,2},{4,3},{5,4},{6,5},{7,6},{9,8},{10,9},{11,10},{12... | collective-permute-start | bytes 4718600 | tf_op jit(solution)/shard_map/ppermute | solution.py:378
  7.1 39.5 %collective-permute-start.1 = (f32[2,256,512]{2,1,0:T(8,128)S(1)}, f32[2,256,512]{2,1,0:T(8,128)S(1)}, u32[]{:S(2)}, u32[]{:S(2)}) collective-permute-start(f32[2,256,512]{2,1,0:T(8,128)S(1)} %slice.20), channel_id=1, source_target_pairs={{8,0},{9,1},{10,2},{11,3},{12,4},{13,5},{14,6},{15,7},{16,8},{17,9... | collective-permute-start | bytes 3145736 | tf_op jit(solution)/shard_map/ppermute | solution.py:378
  9.5 37.1 %collective-permute-start.2 = (f32[2,256,256]{2,1,0:T(8,128)S(1)}, f32[2,256,256]{2,1,0:T(8,128)S(1)}, u32[]{:S(2)}, u32[]{:S(2)}) collective-permute-start(f32[2,256,256]{2,1,0:T(8,128)S(1)} %slice.21), channel_id=1, source_target_pairs={{9,0},{10,1},{11,2},{12,3},{13,4},{14,5},{15,6},{17,8},{18,9},{19,... | collective-permute-start | bytes 1572872 | tf_op jit(solution)/shard_map/ppermute | solution.py:378
  46.5 1.2 copy-start.5
  61.5 115.7 %collective-permute-start.3 = (f32[3,2,768,128]{3,2,1,0:T(8,128)}, f32[3,2,768,128]{3,2,1,0:T(8,128)}, u32[]{:S(2)}, u32[]{:S(2)}) collective-permute-start(f32[3,2,768,128]{3,2,1,0:T(8,128)} %get-tuple-element.12), channel_id=1, source_target_pairs={{0,1},{1,2},{2,3},{3,4},{4,5},{5,6},{6,7},{8,9},{9,10},{10,11},{11... | collective-permute-start | bytes 7077896 | tf_op jit(solution)/shard_map/ppermute | solution.py:378
  77.1 44.0 %all-to-all-start = ((f32[128,12,128]{2,1,0:T(8,128)}), f32[128,12,128]{2,1,0:T(8,128)S(1)}, u32[]{:S(2)}, u32[]{:S(2)}) async-start(f32[128,12,128]{2,1,0:T(8,128)} %get-tuple-element.15), calls=%async_computation | async-start | bytes 2097152 | tf_op jit(solution)/shard_map/all_to_all | solution.py:477
  97.9 79.3 %collective-permute-start.4 = (f32[3,4,256,128]{3,2,1,0:T(8,128)}, f32[3,4,256,128]{3,2,1,0:T(8,128)}, u32[]{:S(2)}, u32[]{:S(2)}) collective-permute-start(f32[3,4,256,128]{3,2,1,0:T(8,128)} %get-tuple-element.13), channel_id=1, source_target_pairs={{0,8},{1,9},{2,10},{3,11},{4,12},{5,13},{6,14},{7,15},{8,16},{9,17... | collective-permute-start | bytes 4718600 | tf_op jit(solution)/shard_map/ppermute | solution.py:378
  102.5 74.7 %collective-permute-start.5 = (f32[3,2,256,128]{3,2,1,0:T(8,128)S(1)}, f32[3,2,256,128]{3,2,1,0:T(8,128)S(1)}, u32[]{:S(2)}, u32[]{:S(2)}) collective-permute-start(f32[3,2,256,128]{3,2,1,0:T(8,128)S(1)} %get-tuple-element.14), channel_id=1, source_target_pairs={{0,9},{1,10},{2,11},{3,12},{4,13},{5,14},{6,15},{8,17},{9,18},{10,... | collective-permute-start | bytes 2359304 | tf_op jit(solution)/shard_map/ppermute | solution.py:378
  177.2 1.0 copy-start.4

commit v3 on v2

--- a/solution.py
+++ b/solution.py
@@ -14,6 +14,7 @@
 ROWS = 768
 COLS = 512
 CAP = 24
+AROUND = ((0, 1), (1, 0), (1, 1))
 CH = 16
 SPARE = ROWS + SIZE
 DEEP = SPARE + SIZE
@@ -89,16 +90,22 @@
     return jnp.where(low_first, ra, rb), jnp.where(low_first, rb, ra)
 
 
-def slots_kernel(inside, *refs):
-    if inside:
-        count_ref, pos_ref, own_ref, amp_ref, probe_ref, left_ref, right_ref = refs[:7]
-        own_out, sums_out = refs[7:9]
-        refs = refs[9:]
+EAST, SOUTH, INSIDE = range(3)
+
+
+def slots_kernel(mode, *refs):
+    count_ref, pos_ref, amp_ref, probe_ref, left_ref, right_ref, own_ref = refs[:7]
+    refs = refs[7:]
+    if mode == EAST:
+        east_ref, own_out, east_out, sums_out = refs[:4]
+        refs = refs[4:]
+    elif mode == SOUTH:
+        east_ref, south_ref, corner_ref, own_in, east_in, sums_in = refs[:6]
+        own_out, east_out, south_out, corner_out, sums_out = refs[6:11]
+        refs = refs[11:]
     else:
-        count_ref, pos_ref, own_ref, east_ref, south_ref, corner_ref, own_in, sums_in = refs[:8]
-        amp_ref, probe_ref, left_ref, right_ref = refs[8:12]
-        own_out, east_out, south_out, corner_out, parts_out = refs[12:17]
-        refs = refs[17:]
+        own_in, sums_in, own_out, parts_out = refs[:4]
+        refs = refs[4:]
     todo, ext, acc, sums, work_a, work_b, amp, piece_sem, acc_sem, amp_sem = refs
 
     pieces = []
@@ -111,29 +118,37 @@
             span = pl.ds(HALF * (t % 4), HALF)
             if t < 4:
                 piece(own_ref.at[c, :, span], c, t, pl.ds(0, ROWS))
-            elif not inside:
+            elif mode != INSIDE:
                 piece(east_ref.at[c, :, span], c, t, pl.ds(0, ROWS))
-            if not inside:
+            if mode == SOUTH:
                 piece((south_ref if t < 4 else corner_ref).at[c, :, span], c, t, pl.ds(ROWS, SIZE))
     for copy in pieces:
         copy.start()
+    main, south, own_tiles, east_tiles = pl.ds(0, ROWS), pl.ds(ROWS, SIZE), pl.ds(0, 4), pl.ds(4, 2)
+    field = pl.ds(0, 2)
+    own_acc = acc.at[:, own_tiles, main]
+    east_acc = acc.at[field, east_tiles, main]
     earlier = []
-    if not inside:
+    if mode != EAST:
         earlier = [
-            pltpu.make_async_copy(own_in, acc.at[:, pl.ds(0, 4), pl.ds(0, ROWS)], acc_sem.at[0]),
+            pltpu.make_async_copy(own_in, own_acc, acc_sem.at[0]),
             pltpu.make_async_copy(sums_in, sums.at[0], acc_sem.at[1]),
         ]
+    if mode == SOUTH:
+        earlier.append(pltpu.make_async_copy(east_in, east_acc, acc_sem.at[2]))
     for copy in earlier:
         copy.start()
 
     def choose(k, found):
         row = lax.rem(pos_ref[0, k], ROWS)
         col = lax.rem(pos_ref[1, k], COLS)
-        within = jnp.where(row <= ROWS - SIZE, 1, 0) * jnp.where(col <= COLS - SIZE, 1, 0)
+        below = jnp.where(row > ROWS - SIZE, 1, 0)
+        beside = jnp.where(col > COLS - SIZE, 1, 0)
+        ours = (beside * (1 - below), below, (1 - below) * (1 - beside))[mode]
         todo[0, found] = k
         todo[1, found] = row
         todo[2, found] = col
-        return found + (within if inside else 1 - within)
+        return found + ours
 
     count = lax.fori_loop(0, count_ref[0, 0], choose, 0)
     todo[0, count] = 0
@@ -155,12 +170,11 @@
                     copy.start()
 
     fetch(0, 0)
-    if inside:
-        acc[:, :4, :ROWS] = jnp.zeros((3, 4, ROWS, HALF), jnp.float32)
+    if mode == EAST:
+        acc[:, :, :ROWS] = jnp.zeros((3, 6, ROWS, HALF), jnp.float32)
         sums[0] = jnp.zeros((3, 2, SIZE, HALF), jnp.float32)
-    else:
-        acc[:, 4:, :SPARE] = jnp.zeros((3, 2, SPARE, HALF), jnp.float32)
-        acc[:, :4, ROWS:SPARE] = jnp.zeros((3, 4, SIZE, HALF), jnp.float32)
+    elif mode == SOUTH:
+        acc[:, :, ROWS:SPARE] = jnp.zeros((3, 6, SIZE, HALF), jnp.float32)
     for copy in pieces + earlier:
         copy.wait()
     lane = lanes(CH)
@@ -318,17 +332,16 @@
         return carry
 
     lax.fori_loop(0, pairs, body, 0)
-    outs = [pltpu.make_async_copy(acc.at[:, pl.ds(0, 4), pl.ds(0, ROWS)], own_out, acc_sem.at[0])]
-    if inside:
+    outs = [pltpu.make_async_copy(own_acc, own_out, acc_sem.at[0])]
+    if mode != INSIDE:
         outs.append(pltpu.make_async_copy(sums.at[0], sums_out, acc_sem.at[1]))
-    else:
-        south, east = pl.ds(ROWS, SIZE), pl.ds(4, 2)
-        outs.append(pltpu.make_async_copy(acc.at[:, east, pl.ds(0, ROWS)], east_out, acc_sem.at[1]))
-        outs.append(pltpu.make_async_copy(acc.at[:, pl.ds(0, 4), south], south_out, acc_sem.at[2]))
-        outs.append(pltpu.make_async_copy(acc.at[:, east, south], corner_out, acc_sem.at[3]))
+        outs.append(pltpu.make_async_copy(east_acc, east_out, acc_sem.at[2]))
+    if mode == SOUTH:
+        outs.append(pltpu.make_async_copy(acc.at[field, own_tiles, south], south_out, acc_sem.at[3]))
+        outs.append(pltpu.make_async_copy(acc.at[field, east_tiles, south], corner_out, acc_sem.at[4]))
     for copy in outs:
         copy.start()
-    if not inside:
+    if mode == INSIDE:
         for j in range(2):
 
             def arrange(b, carry):
@@ -343,28 +356,70 @@
         copy.wait()
 
 
-def final_kernel(own_ref, acc_ref, right_ref, below_ref, corner_ref, out_ref):
-    tile = pl.program_id(0)
-    block = pl.program_id(1)
-
-    def put(num):
-        den = num[2] + 1.0
+def light_kernel(count_ref, pos_ref, probe_ref, out_ref, todo, power, light):
+    found = 0
+    for n, (down, along) in enumerate(AROUND):
+
+        def choose(k, at):
+            row = lax.rem(pos_ref[n, 0, k], ROWS) - down * ROWS + SIZE
+            col = lax.rem(pos_ref[n, 1, k], COLS) - along * COLS + SIZE
+            todo[0, at] = row
+            todo[1, at] = col
+            return at + jnp.where(row > 0, 1, 0) * jnp.where(col > 0, 1, 0)
+
+        found = lax.fori_loop(0, count_ref[n], choose, found)
+    light[2:6, SIZE : SIZE + ROWS] = jnp.zeros((4, ROWS, HALF), jnp.float32)
+    for j in range(2):
+        re = probe_ref[0, :, HALF * j : HALF * (j + 1)]
+        im = probe_ref[1, :, HALF * j : HALF * (j + 1)]
+        power[j] = re * re + im * im
+
+    def body(k, carry):
+        row, col = todo[0, k], todo[1, k]
+        tile, s = lax.div(col, HALF), lax.rem(col, HALF)
+        ge = lanes(CH) >= s
+        for i in range(0, SIZE, CH):
+            p0, p1 = rolled(power[0, i : i + CH], power[1, i : i + CH], s, ge)
+            at = pl.ds(row + i, CH)
+            new = [
+                light[tile, at, :] + jnp.where(ge, p0, 0.0),
+                light[tile + 1, at, :] + p1,
+                light[tile + 2, at, :] + jnp.where(ge, 0.0, p0),
+            ]
+            for t in range(3):
+                light[tile + t, at, :] = new[t]
+        return carry
+
+    lax.fori_loop(0, found, body, 0)
+    out_ref[...] = light[2:6, SIZE : SIZE + ROWS]
+
+
+def calm_kernel(own_ref, acc_ref, out_ref):
+    den = acc_ref[2, 0] + 1.0
+    for c in range(2):
+        out_ref[c] = own_ref[c] + acc_ref[c, 0] / den
+
+
+def rim_kernel(calm_ref, own_ref, acc_ref, light_ref, right_ref, below_ref, corner_ref, out_ref):
+    step = pl.program_id(0)
+
+    def put(sources):
+        num = [sum((ref[c, 0] for ref in sources[1:]), sources[0][c, 0]) for c in range(2)]
+        den = acc_ref[2, 0] + light_ref[0] + 1.0
         for c in range(2):
             out_ref[c] = own_ref[c] + num[c] / den
 
-    for near in (True, False):
-        for top in (True, False):
-
-            @pl.when(((tile < 2) == near) & ((block == 0) == top))
-            def _():
-                num = [acc_ref[c, 0] for c in range(3)]
-                if near:
-                    num = [num[c] + right_ref[c, 0] for c in range(3)]
-                if top:
-                    num = [num[c] + below_ref[c, 0] for c in range(3)]
-                if near and top:
-                    num = [num[c] + corner_ref[c, 0] for c in range(3)]
-                put(num)
+    @pl.when(step < 2)
+    def _():
+        put((acc_ref, below_ref))
+
+    @pl.when((step >= 2) & (step < 4))
+    def _():
+        put((acc_ref, right_ref, below_ref, corner_ref))
+
+    @pl.when(step >= 4)
+    def _():
+        put((acc_ref, right_ref))
 
 
 def shift(value, down, along):
@@ -394,20 +449,18 @@
     return jax.ShapeDtypeStruct(shape, jnp.float32)
 
 
-def run_slots(inside, inputs):
-    own = floats(3, 4, ROWS, HALF)
-    if inside:
-        out_shape = (own, floats(3, 2, SIZE, HALF))
-        out_specs = (anywhere(), anywhere())
+def run_slots(mode, common, inputs):
+    own, sums = floats(3, 4, ROWS, HALF), floats(3, 2, SIZE, HALF)
+    east, south, corner = floats(2, 2, ROWS, HALF), floats(2, 4, SIZE, HALF), floats(2, 2, SIZE, HALF)
+    if mode == EAST:
+        out_shape = (own, east, sums)
+    elif mode == SOUTH:
+        out_shape = (own, east, south, corner, sums)
     else:
-        out_shape = (
-            own,
-            floats(3, 2, ROWS, HALF),
-            floats(3, 4, SIZE, HALF),
-            floats(3, 2, SIZE, HALF),
-            floats(128, 12, HALF),
-        )
-        out_specs = (anywhere(),) * 4 + (vmem(),)
+        out_shape = (own, floats(128, 12, HALF))
+    out_specs = [anywhere() for _ in out_shape]
+    if mode == INSIDE:
+        out_specs[1] = vmem()
     work = [
         pltpu.VMEM((2, 2 * SIZE, SIZE), jnp.bfloat16),
         pltpu.VMEM((2, SIZE, SIZE), jnp.float32),
@@ -416,12 +469,12 @@
         pltpu.VMEM((2, 2, SIZE, HALF), jnp.float32),
         pltpu.VMEM((2, 2, SIZE, HALF), jnp.float32),
     ]
-    slots = CAP // 3 if inside else CAP * 2 // 3
+    slots = CAP // 3
     return pl.pallas_call(
-        functools.partial(slots_kernel, inside),
+        functools.partial(slots_kernel, mode),
         out_shape=out_shape,
-        in_specs=[smem()] * 2 + [anywhere()] * (len(inputs) - 5) + [vmem()] * 3,
-        out_specs=out_specs,
+        in_specs=[smem()] * 2 + [anywhere()] + [vmem()] * 3 + [anywhere()] * (1 + len(inputs)),
+        out_specs=tuple(out_specs),
         scratch_shapes=[
             pltpu.SMEM((3, 32), jnp.int32),
             pltpu.VMEM((2, 6, DEEP, HALF), jnp.float32),
@@ -431,51 +484,100 @@
             work,
             pltpu.VMEM((4, 2, SIZE, HALF), jnp.float32),
             pltpu.SemaphoreType.DMA((24,)),
-            pltpu.SemaphoreType.DMA((4,)),
+            pltpu.SemaphoreType.DMA((5,)),
             pltpu.SemaphoreType.DMA((4, 2)),
         ],
         compiler_params=pltpu.CompilerParams(vmem_limit_bytes=VMEM_LIMIT),
         cost_estimate=pl.CostEstimate(
             flops=slots * 48 * SIZE**3, bytes_accessed=slots * SIZE * SIZE * 4, transcendentals=slots * SIZE * SIZE
         ),
-        name="slots_inside" if inside else "slots_other",
-    )(*inputs)
-
-
-def finish(object_field, acc, right, below, corner):
-    def right_at(t, i):
-        return 0, jnp.minimum(t, 1), jnp.where(t < 2, i, 2), 0
-
+        name=("slots_east", "slots_south", "slots_inside")[mode],
+    )(*common, *inputs)
+
+
+def update_calm(object_field, acc):
     return pl.pallas_call(
-        final_kernel,
-        grid=(4, 3),
+        calm_kernel,
+        grid=(2, 2),
         out_shape=floats(2, ROWS, COLS),
         in_specs=[
-            pl.BlockSpec((2, SIZE, HALF), lambda t, i: (0, i, t)),
-            pl.BlockSpec((3, 1, SIZE, HALF), lambda t, i: (0, t, i, 0)),
-            pl.BlockSpec((3, 1, SIZE, HALF), right_at),
-            pl.BlockSpec((3, 1, SIZE, HALF), lambda t, i: (0, t, 0, 0)),
-            pl.BlockSpec((3, 1, SIZE, HALF), lambda t, i: (0, jnp.minimum(t, 1), 0, 0)),
+            pl.BlockSpec((2, SIZE, HALF), lambda t, i: (0, i + 1, t + 2)),
+            pl.BlockSpec((3, 1, SIZE, HALF), lambda t, i: (0, t + 2, i + 1, 0)),
         ],
-        out_specs=pl.BlockSpec((2, SIZE, HALF), lambda t, i: (0, i, t)),
-        name="final",
-    )(object_field, acc, right, below, corner)
+        out_specs=pl.BlockSpec((2, SIZE, HALF), lambda t, i: (0, i + 1, t + 2)),
+        cost_estimate=pl.CostEstimate(flops=1 << 20, bytes_accessed=4 << 20, transcendentals=0),
+        name="calm",
+    )(object_field, acc)
+
+
+def update_rim(calm, object_field, acc, light, right, below, corner):
+    def tile(n):
+        return jnp.where(n < 4, 3 - n, lax.div(n - 4, 2))
+
+    def block(n):
+        return jnp.where(n < 4, 0, 1 + lax.rem(n, 2))
+
+    return pl.pallas_call(
+        rim_kernel,
+        grid=(8,),
+        out_shape=floats(2, ROWS, COLS),
+        in_specs=[
+            anywhere(),
+            pl.BlockSpec((2, SIZE, HALF), lambda n: (0, block(n), tile(n))),
+            pl.BlockSpec((3, 1, SIZE, HALF), lambda n: (0, tile(n), block(n), 0)),
+            pl.BlockSpec((1, SIZE, HALF), lambda n: (tile(n), block(n), 0)),
+            pl.BlockSpec((2, 1, SIZE, HALF), lambda n: (0, jnp.minimum(tile(n), 1), block(n), 0)),
+            pl.BlockSpec((2, 1, SIZE, HALF), lambda n: (0, jnp.where(n < 4, 3 - n, 0), 0, 0)),
+            pl.BlockSpec((2, 1, SIZE, HALF), lambda n: (0, jnp.where(n < 3, 1, 0), 0, 0)),
+        ],
+        out_specs=pl.BlockSpec((2, SIZE, HALF), lambda n: (0, block(n), tile(n))),
+        input_output_aliases={0: 0},
+        cost_estimate=pl.CostEstimate(flops=1 << 20, bytes_accessed=20 << 20, transcendentals=0),
+        name="rim",
+    )(calm, object_field, acc, light, right, below, corner)
+
+
+def light_around(slot_counts, pos, probe):
+    table = jnp.concatenate([pos.reshape(1, 2 * CAP), slot_counts], 1)
+    table = jnp.concatenate([shift(table, down, along) for down, along in AROUND], 0)
+    return pl.pallas_call(
+        light_kernel,
+        out_shape=floats(4, ROWS, HALF),
+        in_specs=[smem(), smem(), vmem()],
+        out_specs=vmem(),
+        scratch_shapes=[
+            pltpu.SMEM((2, 80), jnp.int32),
+            pltpu.VMEM((2, SIZE, HALF), jnp.float32),
+            pltpu.VMEM((8, DEEP, HALF), jnp.float32),
+        ],
+        compiler_params=pltpu.CompilerParams(vmem_limit_bytes=VMEM_LIMIT // 2),
+        cost_estimate=pl.CostEstimate(flops=1 << 20, bytes_accessed=8 << 20, transcendentals=0),
+        name="light",
+    )(table[:, 2 * CAP], table[:, : 2 * CAP].reshape(3, 2, CAP), probe)
 
 
 def local(object_field, probe, slot_counts, positions, amplitude):
     pos = positions.reshape(2, CAP)
     amps = amplitude.reshape(CAP, SIZE, SIZE)
     left, right = (jnp.asarray(t) for t in tables())
+    east = shift(object_field[:, :, :SIZE], 0, -1)
     south = shift(object_field[:, :SIZE, :], -1, 0)
-    east = shift(object_field[:, :, :SIZE], 0, -1)
     corner = shift(object_field[:, :SIZE, :SIZE], -1, -1)
-    common = (amps, probe, left, right)
-    own_part, sums = run_slots(True, (slot_counts, pos, object_field) + common)
-    acc, to_right, to_below, to_corner, parts = run_slots(
-        False, (slot_counts, pos, object_field, east, south, corner, own_part, sums) + common
+    common = (slot_counts, pos, amps, probe, left, right, object_field)
+    light = light_around(slot_counts, pos, probe)
+    east, light = lax.optimization_barrier((east, light))
+    own_part, east_part, sums = run_slots(EAST, common, (east,))
+    own_part, to_right, to_below, to_corner, sums = run_slots(
+        SOUTH, common, (east, south, corner, own_part, east_part, sums)
+    )
+    from_left, from_above, from_corner = shift(to_right, 0, 1), shift(to_below, 1, 0), shift(to_corner, 1, 1)
+    acc, parts = run_slots(INSIDE, common, (own_part, sums))
+    calm = update_calm(object_field, acc)
+    parts, from_left, from_above, from_corner = lax.optimization_barrier(
+        (parts, from_left, from_above, from_corner)
     )
     mine = lax.all_to_all(parts, AXES, 0, 0, tiled=True).sum(0).reshape(3, 4, HALF)
-    new_object = finish(object_field, acc, shift(to_right, 0, 1), shift(to_below, 1, 0), shift(to_corner, 1, 1))
+    new_object = update_rim(calm, object_field, acc, light, from_left, from_above, from_corner)
     me = lax.axis_index(AXES)
     held = lax.dynamic_slice(probe, (0, lax.rem(me, 64) * 4, lax.div(me, 64) * HALF), (2, 4, HALF))
     fresh = (held + mine[:2] / (mine[2][None] + 1.0)).reshape(1, 8, HALF)

time: 190 us -> 166 us (0.87); the launches traced: 188 us -> 166 us
  blocking collectives: 54 us -> 0 us
  Pallas kernels: 28.7 us -> 50.7 us
  starting transfers between devices: 50.6 us -> 63.1 us
  waiting for transfers between devices: 45.2 us -> 37 us
  local copies, waits for them, and re-layouts: 7.94 us -> 13.6 us
    all_to_all x1 -> x0, blocking collectives: 54 us -> none  [local(): lax.all_to_all(jnp.broadcast_to(fresh, (128, 8, HALF)), AXES, 0, 0, tiled...]
    pallas_call x3 -> x6, Pallas kernels: 28.7 us -> 50.7 us  [the longest x3 38.3 us: run_slots(): pl.pallas_call(functools.partial(slots_kernel, mode), out_shape=out_shape...]
    ppermute x6 -> x9, waiting for transfers between devices: 30.1 us -> 14.9 us  [shift(): return lax.ppermute(value, AXES, pairs)]
    ppermute x6 -> x9, starting transfers between devices: 29.8 us -> 37.6 us  [shift(): return lax.ppermute(value, AXES, pairs)]
    all_to_all x0 -> x1, starting transfers between devices: none -> 4.56 us  [local(): lax.all_to_all(jnp.broadcast_to(fresh, (128, 8, HALF)), AXES, 0, 0, tiled...]
    all_to_all x1, waiting for transfers between devices: 15.1 us -> 19.3 us  [local(): lax.all_to_all(parts, AXES, 0, 0, tiled=True).sum(0).reshape(3, 4, HALF)]
    all_to_all x0 -> x1, waiting for transfers between devices: none -> 2.85 us  [local(): lax.all_to_all(jnp.broadcast_to(fresh, (128, 8, HALF)), AXES, 0, 0, tiled...]
    unnamed x12 -> x22, local copies, waits for them, and re-layouts: 2.16 us -> 4.83 us
  transfers between devices with their start and end apart: 7 -> 11, of which waited for: 2 -> 4; matrix products, arithmetic and copies ran while one was open for 2% -> 2% of each run, Pallas kernels for 3% -> 23%
where the time goes in v3:
time: 166 us
  starting transfers between devices  63.1 us (38%)
  Pallas kernels  50.7 us (31%)
  waiting for transfers between devices  37 us (22%)
  local copies, waits for them, and re-layouts  13.6 us (8%)
    pallas_call x3, Pallas kernels, run_slots(): pl.pallas_call(functools.partial(slots_kernel, mode), out_shape=out_shape...  38.3 us
    ppermute x9, starting transfers between devices, shift(): return lax.ppermute(value, AXES, pairs)  37.6 us
    all_to_all x1, starting transfers between devices, local(): lax.all_to_all(parts, AXES, 0, 0, tiled=True).sum(0).reshape(3, 4, HALF)  21 us
    all_to_all x1, waiting for transfers between devices, local(): lax.all_to_all(parts, AXES, 0, 0, tiled=True).sum(0).reshape(3, 4, HALF)  19.3 us
    ppermute x9, waiting for transfers between devices, shift(): return lax.ppermute(value, AXES, pairs)  14.9 us
    pallas_call x1, Pallas kernels, update_rim(): pl.pallas_call(rim_kernel, grid=(8,), out_shape=floats(2, ROWS, COLS), in...  7.26 us
    unnamed x22, local copies, waits for them, and re-layouts  4.83 us
    all_to_all x1, starting transfers between devices, local(): lax.all_to_all(jnp.broadcast_to(fresh, (128, 8, HALF)), AXES, 0, 0, tiled...  4.56 us
  transfers between devices with their start and end apart: 11, of which 4 were waited for; matrix products, arithmetic and copies ran while one was open for 2% of the time, Pallas kernels for 23%

profile of v3, /device:TPU:1, one launch (start us, length us, event | category | flops | bytes accessed | tf_op | source)
XLA Modules:
  0.0 166.3 jit_solution(9973266998543086338)
XLA Ops:
  0.6 2.7 %slice.25 = f32[2,768,256]{2,1,0:T(8,128)} slice(f32[2,768,512]{2,1,0:T(8,128)} %own_ref.3), slice={[0:2], [0:768], [0:256]} | slice | bytes 3145728 | tf_op jit(solution)/shard_map/slice | solution.py:563
  3.3 0.0 copy-start.2
  3.3 0.0 copy-start.1
  3.3 3.5 %collective-permute-start = (f32[2,768,256]{2,1,0:T(8,128)}, f32[2,768,256]{2,1,0:T(8,128)}, u32[]{:S(2)}, u32[]{:S(2)}) collective-permute-start(f32[2,768,256]{2,1,0:T(8,128)} %slice.25), channel_id=1, source_target_pairs={{1,0},{2,1},{3,2},{4,3},{5,4},{6,5},{7,6},{9,8},{10,9},{11,10},{12... | collective-permute-start | bytes 4718600 | tf_op jit(solution)/shard_map/ppermute | solution.py:433
  6.7 1.3 slice.28
  8.0 1.3 collective-permute-start.4
  10.0 0.0 copy-done.2
  10.0 0.1 reshape_reshape.3
  10.1 0.1 pad_add_fusion.1
  10.2 3.5 %collective-permute-start.1 = (s32[1,49]{1,0:T(1,128)S(1)}, s32[1,49]{1,0:T(1,128)S(1)}, u32[]{:S(2)}, u32[]{:S(2)}) collective-permute-start(s32[1,49]{1,0:T(1,128)S(1)} %pad_add_fusion.1), channel_id=1, source_target_pairs={{0,1},{1,2},{2,3},{3,4},{4,5},{5,6},{6,7},{8,9},{9,10},{10,11},{11... | collective-permute-start | bytes 596 | tf_op jit(solution)/shard_map/ppermute | solution.py:433
  13.7 4.3 %collective-permute-start.2 = (s32[1,49]{1,0:T(1,128)S(1)}, s32[1,49]{1,0:T(1,128)S(1)}, u32[]{:S(2)}, u32[]{:S(2)}) collective-permute-start(s32[1,49]{1,0:T(1,128)S(1)} %pad_add_fusion.1), channel_id=1, source_target_pairs={{0,8},{1,9},{2,10},{3,11},{4,12},{5,13},{6,14},{7,15},{8,16},{9,17... | collective-permute-start | bytes 596 | tf_op jit(solution)/shard_map/ppermute | solution.py:433
  18.0 3.4 %collective-permute-start.3 = (s32[1,49]{1,0:T(1,128)S(1)}, s32[1,49]{1,0:T(1,128)S(1)}, u32[]{:S(2)}, u32[]{:S(2)}) collective-permute-start(s32[1,49]{1,0:T(1,128)S(1)} %pad_add_fusion.1), channel_id=1, source_target_pairs={{0,9},{1,10},{2,11},{3,12},{4,13},{5,14},{6,15},{8,17},{9,18},{10,... | collective-permute-start | bytes 596 | tf_op jit(solution)/shard_map/ppermute | solution.py:433
  21.4 1.9 %slice.29 = f32[2,256,256]{2,1,0:T(8,128)} slice(f32[2,768,512]{2,1,0:T(8,128)} %own_ref.3), slice={[0:2], [0:256], [0:256]} | slice | bytes 1048576 | tf_op jit(solution)/shard_map/slice | solution.py:565
  23.3 0.0 collective-permute-done.1
  23.3 1.3 collective-permute-start.5
  24.6 0.0 collective-permute-done.2
  24.6 0.0 collective-permute-done.3
  24.6 0.1 reshape.28.pos_ref
  24.7 0.0 copy-start.3
  24.7 0.2 slice_reduce_fusion.count_ref
  24.9 0.0 copy-done.1
  24.9 1.5 light.1.light_ref
  26.3 0.0 copy-start
  26.4 1.1 copy-done
  27.5 0.0 collective-permute-done.refs_7_
  27.5 0.0 copy-done.3
  27.5 0.0 copy-start.5
  27.5 1.4 copy-done.5
  28.9 11.9 %slots_east.1 = (f32[3,4,768,128]{3,2,1,0:T(8,128)}, f32[2,2,768,128]{3,2,1,0:T(8,128)S(1)}, f32[3,2,256,128]{3,2,1,0:T(8,128)S(1)}) custom-call(s32[1,1]{1,0:T(1,128)S(6)} %copy.14.refs_0_, s32[2,24]{1,0:T(2,128)S(1)} %bitcast.8, f32[24,256,256]{2,1,0:T(8,128)} %bitcast.15, f32[2,256,256]{2,1,0:T(8,128)S(1)} %copy-done.1, ...), custom_call_target="tpu_custom_call" | custom-call | flops 6442450944 | bytes 2097152 | tf_op jit(solution)/shard_map/slots_east/pallas_call | solution.py:473
  40.8 0.0 copy-start.7
  40.8 1.1 copy-done.7
  42.0 5.5 %collective-permute-done.5.refs_9_ = f32[2,256,256]{2,1,0:T(8,128)S(1)} collective-permute-done((f32[2,256,256]{2,1,0:T(8,128)}, f32[2,256,256]{2,1,0:T(8,128)S(1)}, u32[]{:S(2)}, u32[]{:S(2)}) %collective-permute-start.5) | collective-permute-done | bytes 524320 | tf_op jit(solution)/shard_map/ppermute | solution.py:433
  47.5 0.0 collective-permute-done.4.refs_8_
  47.5 0.0 copy-start.4
  47.5 0.0 copy-start.6
  47.5 12.5 %slots_south.1 = (f32[3,4,768,128]{3,2,1,0:T(8,128)}, f32[2,2,768,128]{3,2,1,0:T(8,128)}, f32[2,4,256,128]{3,2,1,0:T(8,128)S(1)}, f32[2,2,256,128]{3,2,1,0:T(8,128)S(1)}, f32[3,2,256,128]{3,2,1,0:T(8,128)S(1)}) custom-call(s32[1,1]{1,0:T(1,128)S(6)} %copy.14.refs_0_, s32[2,24]{1,0:T(2,128)S(1)} %bitcast.9, f32[24,256,256]{2,1,0:T(8,128)} %bitcast.16, ...), custom_call_target="tpu_custom_call" | custom-call | flops 6442450944 | bytes 2097152 | tf_op jit(solution)/shard_map/slots_south/pallas_call | solution.py:473
  60.0 1.9 %collective-permute-start.6 = (f32[2,2,768,128]{3,2,1,0:T(8,128)}, f32[2,2,768,128]{3,2,1,0:T(8,128)S(1)}, u32[]{:S(2)}, u32[]{:S(2)}) collective-permute-start(f32[2,2,768,128]{3,2,1,0:T(8,128)} %get-tuple-element.27), channel_id=1, source_target_pairs={{0,1},{1,2},{2,3},{3,4},{4,5},{5,6},{6,7},{8,9},{9,10},{10,11},{11... | collective-permute-start | bytes 4718600 | tf_op jit(solution)/shard_map/ppermute | solution.py:433
  61.9 8.6 %collective-permute-start.7 = (f32[2,4,256,128]{3,2,1,0:T(8,128)S(1)}, f32[2,4,256,128]{3,2,1,0:T(8,128)S(1)}, u32[]{:S(2)}, u32[]{:S(2)}) collective-permute-start(f32[2,4,256,128]{3,2,1,0:T(8,128)S(1)} %get-tuple-element.28), channel_id=1, source_target_pairs={{0,8},{1,9},{2,10},{3,11},{4,12},{5,13},{6,14},{7,15},{8,16},{9,17... | collective-permute-start | bytes 3145736 | tf_op jit(solution)/shard_map/ppermute | solution.py:433
  70.6 9.8 %collective-permute-start.8 = (f32[2,2,256,128]{3,2,1,0:T(8,128)S(1)}, f32[2,2,256,128]{3,2,1,0:T(8,128)S(1)}, u32[]{:S(2)}, u32[]{:S(2)}) collective-permute-start(f32[2,2,256,128]{3,2,1,0:T(8,128)S(1)} %get-tuple-element.29), channel_id=1, source_target_pairs={{0,9},{1,10},{2,11},{3,12},{4,13},{5,14},{6,15},{8,17},{9,18},{10,... | collective-permute-start | bytes 1572872 | tf_op jit(solution)/shard_map/ppermute | solution.py:433
  80.4 0.0 copy-done.4
  80.4 0.0 copy-done.6
  80.4 13.9 %slots_inside.1 = (f32[3,4,768,128]{3,2,1,0:T(8,128)}, f32[128,12,128]{2,1,0:T(8,128)}) custom-call(s32[1,1]{1,0:T(1,128)S(6)} %copy.14.refs_0_, s32[2,24]{1,0:T(2,128)S(1)} %bitcast.10, f32[24,256,256]{2,1,0:T(8,128)} %bitcast.17, f32[2,256,256]{2,1,0:T(8,128)S(1)} %copy-done.1, bf16[4,256,768]{2,1,0:T(8,128)(2,1)S(1)} %copy-done.4, ...), custom_call_target="tpu_custom_call" | custom-call | flops 6442450944 | bytes 2097152 | tf_op jit(solution)/shard_map/slots_inside/pallas_call | solution.py:473
  94.3 9.4 %collective-permute-done.8.corner_ref = f32[2,2,256,128]{3,2,1,0:T(8,128)S(1)} collective-permute-done((f32[2,2,256,128]{3,2,1,0:T(8,128)S(1)}, f32[2,2,256,128]{3,2,1,0:T(8,128)S(1)}, u32[]{:S(2)}, u32[]{:S(2)}) %collective-permute-start.8) | collective-permute-done | bytes 524320 | tf_op jit(solution)/shard_map/ppermute | solution.py:433
  103.6 0.0 copy-start.10
  103.6 0.0 collective-permute-done.7.below_ref
  103.6 0.0 copy-start.9
  103.7 0.0 collective-permute-done.6.right_ref
  103.7 1.0 copy-done.9
  104.7 0.0 copy-start.8
  104.7 0.1 copy-done.10
  104.8 21.0 %all-to-all-start = ((f32[128,12,128]{2,1,0:T(8,128)}), f32[128,12,128]{2,1,0:T(8,128)S(1)}, u32[]{:S(2)}, u32[]{:S(2)}) async-start(f32[128,12,128]{2,1,0:T(8,128)} %get-tuple-element.33), calls=%async_computation | async-start | bytes 2097152 | tf_op jit(solution)/shard_map/all_to_all | solution.py:579
  125.8 19.3 %all-to-all-done = f32[128,12,128]{2,1,0:T(8,128)S(1)} async-done(((f32[128,12,128]{2,1,0:T(8,128)}), f32[128,12,128]{2,1,0:T(8,128)S(1)}, u32[]{:S(2)}, u32[]{:S(2)}) %all-to-all-start) | async-done | bytes 786464 | tf_op jit(solution)/shard_map/all_to_all | solution.py:579
  145.1 0.1 reduce_sum.9
  145.2 0.0 copy-done.8
  145.2 0.1 divide_add_fusion
  145.3 0.8 broadcast_in_dim.8
  146.2 4.6 %all-to-all-start.1 = ((f32[128,8,128]{2,1,0:T(8,128)}), f32[128,8,128]{2,1,0:T(8,128)S(1)}, u32[]{:S(2)}, u32[]{:S(2)}) async-start(f32[128,8,128]{2,1,0:T(8,128)} %broadcast_in_dim.8), calls=%async_computation.1 | async-start | bytes 1048576 | tf_op jit(solution)/shard_map/all_to_all | solution.py:584
  150.7 3.7 %calm.1.calm_ref = f32[2,768,512]{2,1,0:T(8,128)} custom-call(f32[2,768,512]{2,1,0:T(8,128)} %own_ref.3, f32[3,4,768,128]{3,2,1,0:T(8,128)} %get-tuple-element.24.acc_ref), custom_call_target="tpu_custom_call" | custom-call | flops 1048576 | bytes 4194304 | tf_op jit(solution)/shard_map/calm/pallas_call | solution.py:499
  154.5 7.3 %rim.1 = f32[2,768,512]{2,1,0:T(8,128)} custom-call(f32[2,768,512]{2,1,0:T(8,128)} %calm.1.calm_ref, f32[2,768,512]{2,1,0:T(8,128)} %own_ref.3, f32[3,4,768,128]{3,2,1,0:T(8,128)} %get-tuple-element.24.acc_ref, f32[4,768,128]{2,1,0:T(8,128)} %copy-done, f32[2,2,768,128]{3,2,1,0:T(8,128)} %copy-done.8, ...), custom_call_target="tpu_custom_call", output_to_operand_aliasing={{}: (0, {})} | custom-call | flops 1048576 | bytes 20971520 | tf_op jit(solution)/shard_map/rim/pallas_call | solution.py:520
  161.7 2.9 %all-to-all-done.1 = f32[128,8,128]{2,1,0:T(8,128)S(1)} async-done(((f32[128,8,128]{2,1,0:T(8,128)}), f32[128,8,128]{2,1,0:T(8,128)S(1)}, u32[]{:S(2)}, u32[]{:S(2)}) %all-to-all-start.1) | async-done | bytes 524320 | tf_op jit(solution)/shard_map/all_to_all | solution.py:584
  164.6 0.1 copy.11
  164.7 0.4 copy.12
  165.1 1.2 reshape.30
  (3 shorter events, 0.0 us)
Async XLA Ops:
  3.3 6.7 %copy-start.2 = (s32[1,1,2,24]{3,2,1,0:T(2,128)S(1)}, s32[1,1,2,24]{3,2,1,0:T(2,128)}, u32[]{:S(2)}) copy-start(s32[1,1,2,24]{3,2,1,0:T(2,128)} %param.10) | copy-start | bytes 580
  3.3 21.6 %copy-start.1 = (f32[2,256,256]{2,1,0:T(8,128)S(1)}, f32[2,256,256]{2,1,0:T(8,128)}, u32[]{:S(2)}) copy-start(f32[2,256,256]{2,1,0:T(8,128)} %refs_3_.5) | copy-start | bytes 1572868
  3.3 24.2 %collective-permute-start = (f32[2,768,256]{2,1,0:T(8,128)}, f32[2,768,256]{2,1,0:T(8,128)}, u32[]{:S(2)}, u32[]{:S(2)}) collective-permute-start(f32[2,768,256]{2,1,0:T(8,128)} %slice.25), channel_id=1, source_target_pairs={{1,0},{2,1},{3,2},{4,3},{5,4},{6,5},{7,6},{9,8},{10,9},{11,10},{12... | collective-permute-start | bytes 4718600 | tf_op jit(solution)/shard_map/ppermute | solution.py:433
  8.0 39.5 %collective-permute-start.4 = (f32[2,256,512]{2,1,0:T(8,128)S(1)}, f32[2,256,512]{2,1,0:T(8,128)S(1)}, u32[]{:S(2)}, u32[]{:S(2)}) collective-permute-start(f32[2,256,512]{2,1,0:T(8,128)S(1)} %slice.28), channel_id=1, source_target_pairs={{8,0},{9,1},{10,2},{11,3},{12,4},{13,5},{14,6},{15,7},{16,8},{17,9... | collective-permute-start | bytes 3145736 | tf_op jit(solution)/shard_map/ppermute | solution.py:433
  10.2 13.1 %collective-permute-start.1 = (s32[1,49]{1,0:T(1,128)S(1)}, s32[1,49]{1,0:T(1,128)S(1)}, u32[]{:S(2)}, u32[]{:S(2)}) collective-permute-start(s32[1,49]{1,0:T(1,128)S(1)} %pad_add_fusion.1), channel_id=1, source_target_pairs={{0,1},{1,2},{2,3},{3,4},{4,5},{5,6},{6,7},{8,9},{9,10},{10,11},{11... | collective-permute-start | bytes 596 | tf_op jit(solution)/shard_map/ppermute | solution.py:433
  13.7 10.9 %collective-permute-start.2 = (s32[1,49]{1,0:T(1,128)S(1)}, s32[1,49]{1,0:T(1,128)S(1)}, u32[]{:S(2)}, u32[]{:S(2)}) collective-permute-start(s32[1,49]{1,0:T(1,128)S(1)} %pad_add_fusion.1), channel_id=1, source_target_pairs={{0,8},{1,9},{2,10},{3,11},{4,12},{5,13},{6,14},{7,15},{8,16},{9,17... | collective-permute-start | bytes 596 | tf_op jit(solution)/shard_map/ppermute | solution.py:433
  18.0 6.6 %collective-permute-start.3 = (s32[1,49]{1,0:T(1,128)S(1)}, s32[1,49]{1,0:T(1,128)S(1)}, u32[]{:S(2)}, u32[]{:S(2)}) collective-permute-start(s32[1,49]{1,0:T(1,128)S(1)} %pad_add_fusion.1), channel_id=1, source_target_pairs={{0,9},{1,10},{2,11},{3,12},{4,13},{5,14},{6,15},{8,17},{9,18},{10,... | collective-permute-start | bytes 596 | tf_op jit(solution)/shard_map/ppermute | solution.py:433
  23.3 24.2 %collective-permute-start.5 = (f32[2,256,256]{2,1,0:T(8,128)}, f32[2,256,256]{2,1,0:T(8,128)S(1)}, u32[]{:S(2)}, u32[]{:S(2)}) collective-permute-start(f32[2,256,256]{2,1,0:T(8,128)} %slice.29), channel_id=1, source_target_pairs={{9,0},{10,1},{11,2},{12,3},{13,4},{14,5},{15,6},{17,8},{18,9},{19,... | collective-permute-start | bytes 1572872 | tf_op jit(solution)/shard_map/ppermute | solution.py:433
  24.7 2.8 %copy-start.3 = (bf16[4,256,768]{2,1,0:T(8,128)(2,1)S(1)}, bf16[4,256,768]{2,1,0:T(8,128)(2,1)}, u32[]{:S(2)}) copy-start(bf16[4,256,768]{2,1,0:T(8,128)(2,1)} %constant.34.clone.refs_4_) | copy-start | bytes 4718596
  26.3 1.1 copy-start
  27.5 1.4 copy-start.5
  40.8 1.1 copy-start.7
  47.5 32.9 %copy-start.4 = (bf16[4,256,768]{2,1,0:T(8,128)(2,1)S(1)}, bf16[4,256,768]{2,1,0:T(8,128)(2,1)}, u32[]{:S(2)}) copy-start(bf16[4,256,768]{2,1,0:T(8,128)(2,1)} %constant.34.clone.refs_4_) | copy-start | bytes 4718596
  47.5 32.9 %copy-start.6 = (bf16[4,768,256]{2,1,0:T(8,128)(2,1)S(1)}, bf16[4,768,256]{2,1,0:T(8,128)(2,1)}, u32[]{:S(2)}) copy-start(bf16[4,768,256]{2,1,0:T(8,128)(2,1)} %constant.35.clone.refs_5_) | copy-start | bytes 4718596
  60.0 43.6 %collective-permute-start.6 = (f32[2,2,768,128]{3,2,1,0:T(8,128)}, f32[2,2,768,128]{3,2,1,0:T(8,128)S(1)}, u32[]{:S(2)}, u32[]{:S(2)}) collective-permute-start(f32[2,2,768,128]{3,2,1,0:T(8,128)} %get-tuple-element.27), channel_id=1, source_target_pairs={{0,1},{1,2},{2,3},{3,4},{4,5},{5,6},{6,7},{8,9},{9,10},{10,11},{11... | collective-permute-start | bytes 4718600 | tf_op jit(solution)/shard_map/ppermute | solution.py:433
  61.9 41.7 %collective-permute-start.7 = (f32[2,4,256,128]{3,2,1,0:T(8,128)S(1)}, f32[2,4,256,128]{3,2,1,0:T(8,128)S(1)}, u32[]{:S(2)}, u32[]{:S(2)}) collective-permute-start(f32[2,4,256,128]{3,2,1,0:T(8,128)S(1)} %get-tuple-element.28), channel_id=1, source_target_pairs={{0,8},{1,9},{2,10},{3,11},{4,12},{5,13},{6,14},{7,15},{8,16},{9,17... | collective-permute-start | bytes 3145736 | tf_op jit(solution)/shard_map/ppermute | solution.py:433
  70.6 33.1 %collective-permute-start.8 = (f32[2,2,256,128]{3,2,1,0:T(8,128)S(1)}, f32[2,2,256,128]{3,2,1,0:T(8,128)S(1)}, u32[]{:S(2)}, u32[]{:S(2)}) collective-permute-start(f32[2,2,256,128]{3,2,1,0:T(8,128)S(1)} %get-tuple-element.29), channel_id=1, source_target_pairs={{0,9},{1,10},{2,11},{3,12},{4,13},{5,14},{6,15},{8,17},{9,18},{10,... | collective-permute-start | bytes 1572872 | tf_op jit(solution)/shard_map/ppermute | solution.py:433
  103.6 1.1 copy-start.10
  103.6 1.0 copy-start.9
  104.7 40.6 %copy-start.8 = (f32[2,2,768,128]{3,2,1,0:T(8,128)}, f32[2,2,768,128]{3,2,1,0:T(8,128)S(1)}, u32[]{:S(2)}) copy-start(f32[2,2,768,128]{3,2,1,0:T(8,128)S(1)} %collective-permute-done.6.right_ref) | copy-start | bytes 4718596
  104.8 40.3 %all-to-all-start = ((f32[128,12,128]{2,1,0:T(8,128)}), f32[128,12,128]{2,1,0:T(8,128)S(1)}, u32[]{:S(2)}, u32[]{:S(2)}) async-start(f32[128,12,128]{2,1,0:T(8,128)} %get-tuple-element.33), calls=%async_computation | async-start | bytes 2097152 | tf_op jit(solution)/shard_map/all_to_all | solution.py:579
  146.2 18.4 %all-to-all-start.1 = ((f32[128,8,128]{2,1,0:T(8,128)}), f32[128,8,128]{2,1,0:T(8,128)S(1)}, u32[]{:S(2)}, u32[]{:S(2)}) async-start(f32[128,8,128]{2,1,0:T(8,128)} %broadcast_in_dim.8), calls=%async_computation.1 | async-start | bytes 1048576 | tf_op jit(solution)/shard_map/all_to_all | solution.py:584

commit v4 on v3

--- a/solution.py
+++ b/solution.py
@@ -573,8 +573,8 @@
     from_left, from_above, from_corner = shift(to_right, 0, 1), shift(to_below, 1, 0), shift(to_corner, 1, 1)
     acc, parts = run_slots(INSIDE, common, (own_part, sums))
     calm = update_calm(object_field, acc)
-    parts, from_left, from_above, from_corner = lax.optimization_barrier(
-        (parts, from_left, from_above, from_corner)
+    parts, calm, from_left, from_above, from_corner = lax.optimization_barrier(
+        (parts, calm, from_left, from_above, from_corner)
     )
     mine = lax.all_to_all(parts, AXES, 0, 0, tiled=True).sum(0).reshape(3, 4, HALF)
     new_object = update_rim(calm, object_field, acc, light, from_left, from_above, from_corner)

time: 166 us -> 169 us (1.018); the launches traced: 166 us -> 166 us
  waiting for transfers between devices: 37 us -> 48.4 us
  Pallas kernels: 50.7 us -> 45.4 us
  starting transfers between devices: 63.1 us -> 57.9 us
    ppermute x9, waiting for transfers between devices: 14.9 us -> 22.6 us  [shift(): return lax.ppermute(value, AXES, pairs)]
    pallas_call x3, Pallas kernels: 38.3 us -> 32.2 us  [run_slots(): pl.pallas_call(functools.partial(slots_kernel, mode), out_shape=out_shape...]
    ppermute x9, starting transfers between devices: 37.6 us -> 31.4 us  [shift(): return lax.ppermute(value, AXES, pairs)]
    all_to_all x1, waiting for transfers between devices: 2.85 us -> 6.55 us  [local(): lax.all_to_all(jnp.broadcast_to(fresh, (128, 8, HALF)), AXES, 0, 0, tiled...]
    unnamed x22 -> x18, local copies, waits for them, and re-layouts: 4.83 us -> 3.7 us
  transfers between devices with their start and end apart: 11 -> 11, of which waited for: 4 -> 4; matrix products, arithmetic and copies ran while one was open for 2% -> 2% of each run, Pallas kernels for 23% -> 18%
where the time goes in v4:
time: 169 us; the launch traced here: 166 us
  starting transfers between devices  57.9 us (34%)
  waiting for transfers between devices  48.4 us (29%)
  Pallas kernels  45.4 us (27%)
  local copies, waits for them, and re-layouts  12.5 us (7%)
    pallas_call x3, Pallas kernels, run_slots(): pl.pallas_call(functools.partial(slots_kernel, mode), out_shape=out_shape...  32.2 us
    ppermute x9, starting transfers between devices, shift(): return lax.ppermute(value, AXES, pairs)  31.4 us
    ppermute x9, waiting for transfers between devices, shift(): return lax.ppermute(value, AXES, pairs)  22.6 us
    all_to_all x1, starting transfers between devices, local(): lax.all_to_all(parts, AXES, 0, 0, tiled=True).sum(0).reshape(3, 4, HALF)  21.9 us
    all_to_all x1, waiting for transfers between devices, local(): lax.all_to_all(parts, AXES, 0, 0, tiled=True).sum(0).reshape(3, 4, HALF)  19.3 us
    pallas_call x1, Pallas kernels, update_rim(): pl.pallas_call(rim_kernel, grid=(8,), out_shape=floats(2, ROWS, COLS), in...  7.27 us
    all_to_all x1, waiting for transfers between devices, local(): lax.all_to_all(jnp.broadcast_to(fresh, (128, 8, HALF)), AXES, 0, 0, tiled...  6.55 us
    all_to_all x1, starting transfers between devices, local(): lax.all_to_all(jnp.broadcast_to(fresh, (128, 8, HALF)), AXES, 0, 0, tiled...  4.57 us
  transfers between devices with their start and end apart: 11, of which 4 were waited for; matrix products, arithmetic and copies ran while one was open for 2% of the time, Pallas kernels for 18%

profile of v4, /device:TPU:1, one launch (start us, length us, event | category | flops | bytes accessed | tf_op | source)
XLA Modules:
  0.0 166.0 jit_solution(11241512836848989422)
XLA Ops:
  0.6 2.7 %slice.25 = f32[2,768,256]{2,1,0:T(8,128)} slice(f32[2,768,512]{2,1,0:T(8,128)} %own_ref.3), slice={[0:2], [0:768], [0:256]} | slice | bytes 3145728 | tf_op jit(solution)/shard_map/slice | solution.py:563
  3.3 0.0 copy-start.2
  3.3 0.0 copy-start.1
  3.3 3.5 %collective-permute-start = (f32[2,768,256]{2,1,0:T(8,128)}, f32[2,768,256]{2,1,0:T(8,128)}, u32[]{:S(2)}, u32[]{:S(2)}) collective-permute-start(f32[2,768,256]{2,1,0:T(8,128)} %slice.25), channel_id=1, source_target_pairs={{1,0},{2,1},{3,2},{4,3},{5,4},{6,5},{7,6},{9,8},{10,9},{11,10},{12... | collective-permute-start | bytes 4718600 | tf_op jit(solution)/shard_map/ppermute | solution.py:433
  6.7 1.3 slice.28
  8.0 1.3 collective-permute-start.4
  10.0 0.0 copy-done.2
  10.0 0.1 reshape_reshape.3
  10.1 0.1 pad_add_fusion.1
  10.2 3.5 %collective-permute-start.1 = (s32[1,49]{1,0:T(1,128)S(1)}, s32[1,49]{1,0:T(1,128)S(1)}, u32[]{:S(2)}, u32[]{:S(2)}) collective-permute-start(s32[1,49]{1,0:T(1,128)S(1)} %pad_add_fusion.1), channel_id=1, source_target_pairs={{0,1},{1,2},{2,3},{3,4},{4,5},{5,6},{6,7},{8,9},{9,10},{10,11},{11... | collective-permute-start | bytes 596 | tf_op jit(solution)/shard_map/ppermute | solution.py:433
  13.7 4.3 %collective-permute-start.2 = (s32[1,49]{1,0:T(1,128)S(1)}, s32[1,49]{1,0:T(1,128)S(1)}, u32[]{:S(2)}, u32[]{:S(2)}) collective-permute-start(s32[1,49]{1,0:T(1,128)S(1)} %pad_add_fusion.1), channel_id=1, source_target_pairs={{0,8},{1,9},{2,10},{3,11},{4,12},{5,13},{6,14},{7,15},{8,16},{9,17... | collective-permute-start | bytes 596 | tf_op jit(solution)/shard_map/ppermute | solution.py:433
  18.0 3.4 %collective-permute-start.3 = (s32[1,49]{1,0:T(1,128)S(1)}, s32[1,49]{1,0:T(1,128)S(1)}, u32[]{:S(2)}, u32[]{:S(2)}) collective-permute-start(s32[1,49]{1,0:T(1,128)S(1)} %pad_add_fusion.1), channel_id=1, source_target_pairs={{0,9},{1,10},{2,11},{3,12},{4,13},{5,14},{6,15},{8,17},{9,18},{10,... | collective-permute-start | bytes 596 | tf_op jit(solution)/shard_map/ppermute | solution.py:433
  21.4 1.9 %slice.29 = f32[2,256,256]{2,1,0:T(8,128)} slice(f32[2,768,512]{2,1,0:T(8,128)} %own_ref.3), slice={[0:2], [0:256], [0:256]} | slice | bytes 1048576 | tf_op jit(solution)/shard_map/slice | solution.py:565
  23.3 0.0 collective-permute-done.1
  23.3 1.3 collective-permute-start.5
  24.6 0.0 collective-permute-done.2
  24.6 0.0 collective-permute-done.3
  24.6 0.1 reshape.28.pos_ref
  24.7 0.0 copy-start.3
  24.7 0.2 slice_reduce_fusion.count_ref
  24.9 0.0 copy-done.1
  24.9 2.3 %light.1.light_ref = f32[4,768,128]{2,1,0:T(8,128)S(1)} custom-call(s32[3]{0:T(128)S(1)} %slice_reduce_fusion.count_ref, s32[3,2,24]{2,1,0:T(2,128)S(1)} %reshape.28.pos_ref, f32[2,256,256]{2,1,0:T(8,128)S(1)} %copy-done.1), custom_call_target="tpu_custom_call" | custom-call | flops 1048576 | bytes 8388608 | tf_op jit(solution)/shard_map/light/pallas_call | solution.py:543
  27.2 0.0 copy-start
  27.2 1.1 copy-done
  28.3 0.0 collective-permute-done.refs_7_
  28.3 0.0 copy-done.3
  28.3 0.0 copy-start.5
  28.3 1.4 copy-done.5
  29.7 8.7 %slots_east.1 = (f32[3,4,768,128]{3,2,1,0:T(8,128)}, f32[2,2,768,128]{3,2,1,0:T(8,128)S(1)}, f32[3,2,256,128]{3,2,1,0:T(8,128)S(1)}) custom-call(s32[1,1]{1,0:T(1,128)S(6)} %copy.14.refs_0_, s32[2,24]{1,0:T(2,128)S(1)} %bitcast.8, f32[24,256,256]{2,1,0:T(8,128)} %bitcast.15, f32[2,256,256]{2,1,0:T(8,128)S(1)} %copy-done.1, ...), custom_call_target="tpu_custom_call" | custom-call | flops 6442450944 | bytes 2097152 | tf_op jit(solution)/shard_map/slots_east/pallas_call | solution.py:473
  38.4 0.0 copy-start.7
  38.4 1.1 copy-done.7
  39.5 8.0 %collective-permute-done.5.refs_9_ = f32[2,256,256]{2,1,0:T(8,128)S(1)} collective-permute-done((f32[2,256,256]{2,1,0:T(8,128)}, f32[2,256,256]{2,1,0:T(8,128)S(1)}, u32[]{:S(2)}, u32[]{:S(2)}) %collective-permute-start.5) | collective-permute-done | bytes 524320 | tf_op jit(solution)/shard_map/ppermute | solution.py:433
  47.5 0.0 collective-permute-done.4.refs_8_
  47.5 0.0 copy-start.4
  47.5 0.0 copy-start.6
  47.5 16.1 %slots_south.1 = (f32[3,4,768,128]{3,2,1,0:T(8,128)}, f32[2,2,768,128]{3,2,1,0:T(8,128)}, f32[2,4,256,128]{3,2,1,0:T(8,128)S(1)}, f32[2,2,256,128]{3,2,1,0:T(8,128)}, f32[3,2,256,128]{3,2,1,0:T(8,128)S(1)}) custom-call(s32[1,1]{1,0:T(1,128)S(6)} %copy.14.refs_0_, s32[2,24]{1,0:T(2,128)S(1)} %bitcast.9, f32[24,256,256]{2,1,0:T(8,128)} %bitcast.16, ...), custom_call_target="tpu_custom_call" | custom-call | flops 6442450944 | bytes 2097152 | tf_op jit(solution)/shard_map/slots_south/pallas_call | solution.py:473
  63.6 5.6 %collective-permute-start.6 = (f32[2,2,768,128]{3,2,1,0:T(8,128)}, f32[2,2,768,128]{3,2,1,0:T(8,128)}, u32[]{:S(2)}, u32[]{:S(2)}) collective-permute-start(f32[2,2,768,128]{3,2,1,0:T(8,128)} %get-tuple-element.27), channel_id=1, source_target_pairs={{0,1},{1,2},{2,3},{3,4},{4,5},{5,6},{6,7},{8,9},{9,10},{10,11},{11... | collective-permute-start | bytes 4718600 | tf_op jit(solution)/shard_map/ppermute | solution.py:433
  69.2 2.3 %collective-permute-start.7 = (f32[2,4,256,128]{3,2,1,0:T(8,128)S(1)}, f32[2,4,256,128]{3,2,1,0:T(8,128)}, u32[]{:S(2)}, u32[]{:S(2)}) collective-permute-start(f32[2,4,256,128]{3,2,1,0:T(8,128)S(1)} %get-tuple-element.28), channel_id=1, source_target_pairs={{0,8},{1,9},{2,10},{3,11},{4,12},{5,13},{6,14},{7,15},{8,16},{9,17... | collective-permute-start | bytes 3145736 | tf_op jit(solution)/shard_map/ppermute | solution.py:433
  71.5 6.3 %collective-permute-start.8 = (f32[2,2,256,128]{3,2,1,0:T(8,128)}, f32[2,2,256,128]{3,2,1,0:T(8,128)S(1)}, u32[]{:S(2)}, u32[]{:S(2)}) collective-permute-start(f32[2,2,256,128]{3,2,1,0:T(8,128)} %get-tuple-element.29), channel_id=1, source_target_pairs={{0,9},{1,10},{2,11},{3,12},{4,13},{5,14},{6,15},{8,17},{9,18},{10,... | collective-permute-start | bytes 1572872 | tf_op jit(solution)/shard_map/ppermute | solution.py:433
  77.8 0.0 copy-done.4
  77.8 0.0 copy-done.6
  77.8 7.4 %slots_inside.1 = (f32[3,4,768,128]{3,2,1,0:T(8,128)}, f32[128,12,128]{2,1,0:T(8,128)}) custom-call(s32[1,1]{1,0:T(1,128)S(6)} %copy.14.refs_0_, s32[2,24]{1,0:T(2,128)S(1)} %bitcast.10, f32[24,256,256]{2,1,0:T(8,128)} %bitcast.17, f32[2,256,256]{2,1,0:T(8,128)S(1)} %copy-done.1, bf16[4,256,768]{2,1,0:T(8,128)(2,1)S(1)} %copy-done.4, ...), custom_call_target="tpu_custom_call" | custom-call | flops 6442450944 | bytes 2097152 | tf_op jit(solution)/shard_map/slots_inside/pallas_call | solution.py:473
  85.3 3.7 %calm.1.calm_ref = f32[2,768,512]{2,1,0:T(8,128)} custom-call(f32[2,768,512]{2,1,0:T(8,128)} %own_ref.3, f32[3,4,768,128]{3,2,1,0:T(8,128)} %get-tuple-element.26.acc_ref), custom_call_target="tpu_custom_call" | custom-call | flops 1048576 | bytes 4194304 | tf_op jit(solution)/shard_map/calm/pallas_call | solution.py:499
  89.0 14.6 %collective-permute-done.8.corner_ref = f32[2,2,256,128]{3,2,1,0:T(8,128)S(1)} collective-permute-done((f32[2,2,256,128]{3,2,1,0:T(8,128)}, f32[2,2,256,128]{3,2,1,0:T(8,128)S(1)}, u32[]{:S(2)}, u32[]{:S(2)}) %collective-permute-start.8) | collective-permute-done | bytes 524320 | tf_op jit(solution)/shard_map/ppermute | solution.py:433
  103.5 0.0 copy-start.8
  103.5 0.0 collective-permute-done.7.below_ref
  103.5 0.0 collective-permute-done.6.right_ref
  103.5 21.9 %all-to-all-start = ((f32[128,12,128]{2,1,0:T(8,128)}), f32[128,12,128]{2,1,0:T(8,128)S(1)}, u32[]{:S(2)}, u32[]{:S(2)}) async-start(f32[128,12,128]{2,1,0:T(8,128)} %get-tuple-element.35), calls=%async_computation | async-start | bytes 2097152 | tf_op jit(solution)/shard_map/all_to_all | solution.py:579
  125.5 19.3 %all-to-all-done = f32[128,12,128]{2,1,0:T(8,128)S(1)} async-done(((f32[128,12,128]{2,1,0:T(8,128)}), f32[128,12,128]{2,1,0:T(8,128)S(1)}, u32[]{:S(2)}, u32[]{:S(2)}) %all-to-all-start) | async-done | bytes 786464 | tf_op jit(solution)/shard_map/all_to_all | solution.py:579
  144.7 0.1 reduce_sum.9
  144.9 0.0 copy-done.8
  144.9 0.1 divide_add_fusion
  145.0 0.9 broadcast_in_dim.8
  145.9 4.6 %all-to-all-start.1 = ((f32[128,8,128]{2,1,0:T(8,128)}), f32[128,8,128]{2,1,0:T(8,128)S(1)}, u32[]{:S(2)}, u32[]{:S(2)}) async-start(f32[128,8,128]{2,1,0:T(8,128)} %broadcast_in_dim.8), calls=%async_computation.1 | async-start | bytes 1048576 | tf_op jit(solution)/shard_map/all_to_all | solution.py:584
  150.5 7.3 %rim.1 = f32[2,768,512]{2,1,0:T(8,128)} custom-call(f32[2,768,512]{2,1,0:T(8,128)} %calm.1.calm_ref, f32[2,768,512]{2,1,0:T(8,128)} %own_ref.3, f32[3,4,768,128]{3,2,1,0:T(8,128)} %get-tuple-element.26.acc_ref, f32[4,768,128]{2,1,0:T(8,128)} %copy-done, f32[2,2,768,128]{3,2,1,0:T(8,128)} %collective-permute-done.6.right_ref, ...), custom_call_target="tpu_custom_call", output_to_operand_aliasing={{}: (0, {})} | custom-call | flops 1048576 | bytes 20971520 | tf_op jit(solution)/shard_map/rim/pallas_call | solution.py:520
  157.7 6.5 %all-to-all-done.1 = f32[128,8,128]{2,1,0:T(8,128)S(1)} async-done(((f32[128,8,128]{2,1,0:T(8,128)}), f32[128,8,128]{2,1,0:T(8,128)S(1)}, u32[]{:S(2)}, u32[]{:S(2)}) %all-to-all-start.1) | async-done | bytes 524320 | tf_op jit(solution)/shard_map/all_to_all | solution.py:584
  164.3 0.1 copy.11
  164.4 0.4 copy.12
  164.8 1.2 reshape.30
  (3 shorter events, 0.0 us)
Async XLA Ops:
  3.3 6.7 %copy-start.2 = (s32[1,1,2,24]{3,2,1,0:T(2,128)S(1)}, s32[1,1,2,24]{3,2,1,0:T(2,128)}, u32[]{:S(2)}) copy-start(s32[1,1,2,24]{3,2,1,0:T(2,128)} %param.10) | copy-start | bytes 580
  3.3 21.6 %copy-start.1 = (f32[2,256,256]{2,1,0:T(8,128)S(1)}, f32[2,256,256]{2,1,0:T(8,128)}, u32[]{:S(2)}) copy-start(f32[2,256,256]{2,1,0:T(8,128)} %refs_3_.5) | copy-start | bytes 1572868
  3.3 25.0 %collective-permute-start = (f32[2,768,256]{2,1,0:T(8,128)}, f32[2,768,256]{2,1,0:T(8,128)}, u32[]{:S(2)}, u32[]{:S(2)}) collective-permute-start(f32[2,768,256]{2,1,0:T(8,128)} %slice.25), channel_id=1, source_target_pairs={{1,0},{2,1},{3,2},{4,3},{5,4},{6,5},{7,6},{9,8},{10,9},{11,10},{12... | collective-permute-start | bytes 4718600 | tf_op jit(solution)/shard_map/ppermute | solution.py:433
  8.0 39.5 %collective-permute-start.4 = (f32[2,256,512]{2,1,0:T(8,128)S(1)}, f32[2,256,512]{2,1,0:T(8,128)S(1)}, u32[]{:S(2)}, u32[]{:S(2)}) collective-permute-start(f32[2,256,512]{2,1,0:T(8,128)S(1)} %slice.28), channel_id=1, source_target_pairs={{8,0},{9,1},{10,2},{11,3},{12,4},{13,5},{14,6},{15,7},{16,8},{17,9... | collective-permute-start | bytes 3145736 | tf_op jit(solution)/shard_map/ppermute | solution.py:433
  10.2 13.1 %collective-permute-start.1 = (s32[1,49]{1,0:T(1,128)S(1)}, s32[1,49]{1,0:T(1,128)S(1)}, u32[]{:S(2)}, u32[]{:S(2)}) collective-permute-start(s32[1,49]{1,0:T(1,128)S(1)} %pad_add_fusion.1), channel_id=1, source_target_pairs={{0,1},{1,2},{2,3},{3,4},{4,5},{5,6},{6,7},{8,9},{9,10},{10,11},{11... | collective-permute-start | bytes 596 | tf_op jit(solution)/shard_map/ppermute | solution.py:433
  13.7 10.9 %collective-permute-start.2 = (s32[1,49]{1,0:T(1,128)S(1)}, s32[1,49]{1,0:T(1,128)S(1)}, u32[]{:S(2)}, u32[]{:S(2)}) collective-permute-start(s32[1,49]{1,0:T(1,128)S(1)} %pad_add_fusion.1), channel_id=1, source_target_pairs={{0,8},{1,9},{2,10},{3,11},{4,12},{5,13},{6,14},{7,15},{8,16},{9,17... | collective-permute-start | bytes 596 | tf_op jit(solution)/shard_map/ppermute | solution.py:433
  18.0 6.6 %collective-permute-start.3 = (s32[1,49]{1,0:T(1,128)S(1)}, s32[1,49]{1,0:T(1,128)S(1)}, u32[]{:S(2)}, u32[]{:S(2)}) collective-permute-start(s32[1,49]{1,0:T(1,128)S(1)} %pad_add_fusion.1), channel_id=1, source_target_pairs={{0,9},{1,10},{2,11},{3,12},{4,13},{5,14},{6,15},{8,17},{9,18},{10,... | collective-permute-start | bytes 596 | tf_op jit(solution)/shard_map/ppermute | solution.py:433
  23.3 24.2 %collective-permute-start.5 = (f32[2,256,256]{2,1,0:T(8,128)}, f32[2,256,256]{2,1,0:T(8,128)S(1)}, u32[]{:S(2)}, u32[]{:S(2)}) collective-permute-start(f32[2,256,256]{2,1,0:T(8,128)} %slice.29), channel_id=1, source_target_pairs={{9,0},{10,1},{11,2},{12,3},{13,4},{14,5},{15,6},{17,8},{18,9},{19,... | collective-permute-start | bytes 1572872 | tf_op jit(solution)/shard_map/ppermute | solution.py:433
  24.7 3.6 %copy-start.3 = (bf16[4,256,768]{2,1,0:T(8,128)(2,1)S(1)}, bf16[4,256,768]{2,1,0:T(8,128)(2,1)}, u32[]{:S(2)}) copy-start(bf16[4,256,768]{2,1,0:T(8,128)(2,1)} %constant.34.clone.refs_4_) | copy-start | bytes 4718596
  27.2 1.1 copy-start
  28.3 1.4 copy-start.5
  38.4 1.1 copy-start.7
  47.5 30.3 %copy-start.4 = (bf16[4,256,768]{2,1,0:T(8,128)(2,1)S(1)}, bf16[4,256,768]{2,1,0:T(8,128)(2,1)}, u32[]{:S(2)}) copy-start(bf16[4,256,768]{2,1,0:T(8,128)(2,1)} %constant.34.clone.refs_4_) | copy-start | bytes 4718596
  47.5 30.3 %copy-start.6 = (bf16[4,768,256]{2,1,0:T(8,128)(2,1)S(1)}, bf16[4,768,256]{2,1,0:T(8,128)(2,1)}, u32[]{:S(2)}) copy-start(bf16[4,768,256]{2,1,0:T(8,128)(2,1)} %constant.35.clone.refs_5_) | copy-start | bytes 4718596
  63.6 40.0 %collective-permute-start.6 = (f32[2,2,768,128]{3,2,1,0:T(8,128)}, f32[2,2,768,128]{3,2,1,0:T(8,128)}, u32[]{:S(2)}, u32[]{:S(2)}) collective-permute-start(f32[2,2,768,128]{3,2,1,0:T(8,128)} %get-tuple-element.27), channel_id=1, source_target_pairs={{0,1},{1,2},{2,3},{3,4},{4,5},{5,6},{6,7},{8,9},{9,10},{10,11},{11... | collective-permute-start | bytes 4718600 | tf_op jit(solution)/shard_map/ppermute | solution.py:433
  69.2 34.3 %collective-permute-start.7 = (f32[2,4,256,128]{3,2,1,0:T(8,128)S(1)}, f32[2,4,256,128]{3,2,1,0:T(8,128)}, u32[]{:S(2)}, u32[]{:S(2)}) collective-permute-start(f32[2,4,256,128]{3,2,1,0:T(8,128)S(1)} %get-tuple-element.28), channel_id=1, source_target_pairs={{0,8},{1,9},{2,10},{3,11},{4,12},{5,13},{6,14},{7,15},{8,16},{9,17... | collective-permute-start | bytes 3145736 | tf_op jit(solution)/shard_map/ppermute | solution.py:433
  71.5 32.0 %collective-permute-start.8 = (f32[2,2,256,128]{3,2,1,0:T(8,128)}, f32[2,2,256,128]{3,2,1,0:T(8,128)S(1)}, u32[]{:S(2)}, u32[]{:S(2)}) collective-permute-start(f32[2,2,256,128]{3,2,1,0:T(8,128)} %get-tuple-element.29), channel_id=1, source_target_pairs={{0,9},{1,10},{2,11},{3,12},{4,13},{5,14},{6,15},{8,17},{9,18},{10,... | collective-permute-start | bytes 1572872 | tf_op jit(solution)/shard_map/ppermute | solution.py:433
  103.5 41.4 %copy-start.8 = (f32[2,2,256,128]{3,2,1,0:T(8,128)}, f32[2,2,256,128]{3,2,1,0:T(8,128)S(1)}, u32[]{:S(2)}) copy-start(f32[2,2,256,128]{3,2,1,0:T(8,128)S(1)} %collective-permute-done.8.corner_ref) | copy-start | bytes 1572868
  103.5 41.2 %all-to-all-start = ((f32[128,12,128]{2,1,0:T(8,128)}), f32[128,12,128]{2,1,0:T(8,128)S(1)}, u32[]{:S(2)}, u32[]{:S(2)}) async-start(f32[128,12,128]{2,1,0:T(8,128)} %get-tuple-element.35), calls=%async_computation | async-start | bytes 2097152 | tf_op jit(solution)/shard_map/all_to_all | solution.py:579
  145.9 18.4 %all-to-all-start.1 = ((f32[128,8,128]{2,1,0:T(8,128)}), f32[128,8,128]{2,1,0:T(8,128)S(1)}, u32[]{:S(2)}, u32[]{:S(2)}) async-start(f32[128,8,128]{2,1,0:T(8,128)} %broadcast_in_dim.8), calls=%async_computation.1 | async-start | bytes 1048576 | tf_op jit(solution)/shard_map/all_to_all | solution.py:584

commit v5 on v4

--- a/solution.py
+++ b/solution.py
@@ -570,7 +570,7 @@
     own_part, to_right, to_below, to_corner, sums = run_slots(
         SOUTH, common, (east, south, corner, own_part, east_part, sums)
     )
-    from_left, from_above, from_corner = shift(to_right, 0, 1), shift(to_below, 1, 0), shift(to_corner, 1, 1)
+    from_above, from_corner, from_left = shift(to_below, 1, 0), shift(to_corner, 1, 1), shift(to_right, 0, 1)
     acc, parts = run_slots(INSIDE, common, (own_part, sums))
     calm = update_calm(object_field, acc)
     parts, calm, from_left, from_above, from_corner = lax.optimization_barrier(

time: 169 us -> 167 us (0.988); the launches traced: 166 us -> 168 us
  Pallas kernels: 45.4 us -> 74.3 us
  waiting for transfers between devices: 48.4 us -> 25.8 us
  starting transfers between devices: 57.9 us -> 53.3 us
    pallas_call x3, Pallas kernels: 32.2 us -> 62 us  [run_slots(): pl.pallas_call(functools.partial(slots_kernel, mode), out_shape=out_shape...]
    ppermute x9, waiting for transfers between devices: 22.6 us -> 0.02 us  [shift(): return lax.ppermute(value, AXES, pairs)]
    all_to_all x1, starting transfers between devices: 21.9 us -> 13.7 us  [local(): lax.all_to_all(parts, AXES, 0, 0, tiled=True).sum(0).reshape(3, 4, HALF)]
    ppermute x9, starting transfers between devices: 31.4 us -> 35 us  [shift(): return lax.ppermute(value, AXES, pairs)]
  transfers between devices with their start and end apart: 11 -> 11, of which waited for: 4 -> 2; matrix products, arithmetic and copies ran while one was open for 2% -> 2% of each run, Pallas kernels for 18% -> 31%
where the time goes in v5:
time: 167 us; the launch traced here: 168 us
  Pallas kernels  74.3 us (44%)
  starting transfers between devices  53.3 us (32%)
  waiting for transfers between devices  25.8 us (15%)
  local copies, waits for them, and re-layouts  12.5 us (7%)
    pallas_call x3, Pallas kernels, run_slots(): pl.pallas_call(functools.partial(slots_kernel, mode), out_shape=out_shape...  62 us
    ppermute x9, starting transfers between devices, shift(): return lax.ppermute(value, AXES, pairs)  35 us
    all_to_all x1, waiting for transfers between devices, local(): lax.all_to_all(parts, AXES, 0, 0, tiled=True).sum(0).reshape(3, 4, HALF)  19.3 us
    all_to_all x1, starting transfers between devices, local(): lax.all_to_all(parts, AXES, 0, 0, tiled=True).sum(0).reshape(3, 4, HALF)  13.7 us
    pallas_call x1, Pallas kernels, update_rim(): pl.pallas_call(rim_kernel, grid=(8,), out_shape=floats(2, ROWS, COLS), in...  7.27 us
    all_to_all x1, waiting for transfers between devices, local(): lax.all_to_all(jnp.broadcast_to(fresh, (128, 8, HALF)), AXES, 0, 0, tiled...  6.55 us
    all_to_all x1, starting transfers between devices, local(): lax.all_to_all(jnp.broadcast_to(fresh, (128, 8, HALF)), AXES, 0, 0, tiled...  4.57 us
    pallas_call x1, Pallas kernels, update_calm(): pl.pallas_call(calm_kernel, grid=(2, 2), out_shape=floats(2, ROWS, COLS),...  3.71 us
  transfers between devices with their start and end apart: 11, of which 2 were waited for; matrix products, arithmetic and copies ran while one was open for 2% of the time, Pallas kernels for 31%

profile of v5, /device:TPU:1, one launch (start us, length us, event | category | flops | bytes accessed | tf_op | source)
XLA Modules:
  0.0 167.8 jit_solution(11241512836848989422)
XLA Ops:
  0.6 2.7 %slice.25 = f32[2,768,256]{2,1,0:T(8,128)} slice(f32[2,768,512]{2,1,0:T(8,128)} %own_ref.3), slice={[0:2], [0:768], [0:256]} | slice | bytes 3145728 | tf_op jit(solution)/shard_map/slice | solution.py:563
  3.3 0.0 copy-start.2
  3.3 0.0 copy-start.1
  3.3 3.5 %collective-permute-start = (f32[2,768,256]{2,1,0:T(8,128)}, f32[2,768,256]{2,1,0:T(8,128)}, u32[]{:S(2)}, u32[]{:S(2)}) collective-permute-start(f32[2,768,256]{2,1,0:T(8,128)} %slice.25), channel_id=1, source_target_pairs={{1,0},{2,1},{3,2},{4,3},{5,4},{6,5},{7,6},{9,8},{10,9},{11,10},{12... | collective-permute-start | bytes 4718600 | tf_op jit(solution)/shard_map/ppermute | solution.py:433
  6.7 1.3 slice.28
  8.0 1.3 collective-permute-start.4
  10.0 0.0 copy-done.2
  10.0 0.1 reshape_reshape.3
  10.1 0.1 pad_add_fusion.1
  10.2 3.5 %collective-permute-start.1 = (s32[1,49]{1,0:T(1,128)S(1)}, s32[1,49]{1,0:T(1,128)S(1)}, u32[]{:S(2)}, u32[]{:S(2)}) collective-permute-start(s32[1,49]{1,0:T(1,128)S(1)} %pad_add_fusion.1), channel_id=1, source_target_pairs={{0,1},{1,2},{2,3},{3,4},{4,5},{5,6},{6,7},{8,9},{9,10},{10,11},{11... | collective-permute-start | bytes 596 | tf_op jit(solution)/shard_map/ppermute | solution.py:433
  13.7 4.3 %collective-permute-start.2 = (s32[1,49]{1,0:T(1,128)S(1)}, s32[1,49]{1,0:T(1,128)S(1)}, u32[]{:S(2)}, u32[]{:S(2)}) collective-permute-start(s32[1,49]{1,0:T(1,128)S(1)} %pad_add_fusion.1), channel_id=1, source_target_pairs={{0,8},{1,9},{2,10},{3,11},{4,12},{5,13},{6,14},{7,15},{8,16},{9,17... | collective-permute-start | bytes 596 | tf_op jit(solution)/shard_map/ppermute | solution.py:433
  18.0 3.4 %collective-permute-start.3 = (s32[1,49]{1,0:T(1,128)S(1)}, s32[1,49]{1,0:T(1,128)S(1)}, u32[]{:S(2)}, u32[]{:S(2)}) collective-permute-start(s32[1,49]{1,0:T(1,128)S(1)} %pad_add_fusion.1), channel_id=1, source_target_pairs={{0,9},{1,10},{2,11},{3,12},{4,13},{5,14},{6,15},{8,17},{9,18},{10,... | collective-permute-start | bytes 596 | tf_op jit(solution)/shard_map/ppermute | solution.py:433
  21.4 1.9 %slice.29 = f32[2,256,256]{2,1,0:T(8,128)} slice(f32[2,768,512]{2,1,0:T(8,128)} %own_ref.3), slice={[0:2], [0:256], [0:256]} | slice | bytes 1048576 | tf_op jit(solution)/shard_map/slice | solution.py:565
  23.3 0.0 collective-permute-done.1
  23.3 1.3 collective-permute-start.5
  24.6 0.0 collective-permute-done.2
  24.6 0.0 collective-permute-done.3
  24.6 0.1 reshape.28.pos_ref
  24.7 0.0 copy-start.3
  24.7 0.2 slice_reduce_fusion.count_ref
  24.9 0.0 copy-done.1
  24.9 1.4 light.1.light_ref
  26.3 0.0 copy-start
  26.3 1.1 copy-done
  27.4 0.0 collective-permute-done.refs_7_
  27.4 0.0 copy-done.3
  27.4 0.0 copy-start.5
  27.4 1.4 copy-done.5
  28.8 18.5 %slots_east.1 = (f32[3,4,768,128]{3,2,1,0:T(8,128)}, f32[2,2,768,128]{3,2,1,0:T(8,128)S(1)}, f32[3,2,256,128]{3,2,1,0:T(8,128)S(1)}) custom-call(s32[1,1]{1,0:T(1,128)S(6)} %copy.14.refs_0_, s32[2,24]{1,0:T(2,128)S(1)} %bitcast.8, f32[24,256,256]{2,1,0:T(8,128)} %bitcast.15, f32[2,256,256]{2,1,0:T(8,128)S(1)} %copy-done.1, ...), custom_call_target="tpu_custom_call" | custom-call | flops 6442450944 | bytes 2097152 | tf_op jit(solution)/shard_map/slots_east/pallas_call | solution.py:473
  47.4 0.0 copy-start.7
  47.4 1.1 copy-done.7
  48.5 0.0 collective-permute-done.5.refs_9_
  48.5 0.0 collective-permute-done.4.refs_8_
  48.5 0.0 copy-start.4
  48.5 0.0 copy-start.6
  48.5 22.7 %slots_south.1 = (f32[3,4,768,128]{3,2,1,0:T(8,128)}, f32[2,2,768,128]{3,2,1,0:T(8,128)}, f32[2,4,256,128]{3,2,1,0:T(8,128)S(1)}, f32[2,2,256,128]{3,2,1,0:T(8,128)}, f32[3,2,256,128]{3,2,1,0:T(8,128)S(1)}) custom-call(s32[1,1]{1,0:T(1,128)S(6)} %copy.14.refs_0_, s32[2,24]{1,0:T(2,128)S(1)} %bitcast.9, f32[24,256,256]{2,1,0:T(8,128)} %bitcast.16, ...), custom_call_target="tpu_custom_call" | custom-call | flops 6442450944 | bytes 2097152 | tf_op jit(solution)/shard_map/slots_south/pallas_call | solution.py:473
  71.3 1.9 %collective-permute-start.6 = (f32[2,2,768,128]{3,2,1,0:T(8,128)}, f32[2,2,768,128]{3,2,1,0:T(8,128)}, u32[]{:S(2)}, u32[]{:S(2)}) collective-permute-start(f32[2,2,768,128]{3,2,1,0:T(8,128)} %get-tuple-element.27), channel_id=1, source_target_pairs={{0,1},{1,2},{2,3},{3,4},{4,5},{5,6},{6,7},{8,9},{9,10},{10,11},{11... | collective-permute-start | bytes 4718600 | tf_op jit(solution)/shard_map/ppermute | solution.py:433
  73.2 2.3 %collective-permute-start.7 = (f32[2,4,256,128]{3,2,1,0:T(8,128)S(1)}, f32[2,4,256,128]{3,2,1,0:T(8,128)}, u32[]{:S(2)}, u32[]{:S(2)}) collective-permute-start(f32[2,4,256,128]{3,2,1,0:T(8,128)S(1)} %get-tuple-element.28), channel_id=1, source_target_pairs={{0,8},{1,9},{2,10},{3,11},{4,12},{5,13},{6,14},{7,15},{8,16},{9,17... | collective-permute-start | bytes 3145736 | tf_op jit(solution)/shard_map/ppermute | solution.py:433
  75.5 13.6 %collective-permute-start.8 = (f32[2,2,256,128]{3,2,1,0:T(8,128)}, f32[2,2,256,128]{3,2,1,0:T(8,128)S(1)}, u32[]{:S(2)}, u32[]{:S(2)}) collective-permute-start(f32[2,2,256,128]{3,2,1,0:T(8,128)} %get-tuple-element.29), channel_id=1, source_target_pairs={{0,9},{1,10},{2,11},{3,12},{4,13},{5,14},{6,15},{8,17},{9,18},{10,... | collective-permute-start | bytes 1572872 | tf_op jit(solution)/shard_map/ppermute | solution.py:433
  89.1 0.0 copy-done.4
  89.1 0.0 copy-done.6
  89.1 20.7 %slots_inside.1 = (f32[3,4,768,128]{3,2,1,0:T(8,128)}, f32[128,12,128]{2,1,0:T(8,128)}) custom-call(s32[1,1]{1,0:T(1,128)S(6)} %copy.14.refs_0_, s32[2,24]{1,0:T(2,128)S(1)} %bitcast.10, f32[24,256,256]{2,1,0:T(8,128)} %bitcast.17, f32[2,256,256]{2,1,0:T(8,128)S(1)} %copy-done.1, bf16[4,256,768]{2,1,0:T(8,128)(2,1)S(1)} %copy-done.4, ...), custom_call_target="tpu_custom_call" | custom-call | flops 6442450944 | bytes 2097152 | tf_op jit(solution)/shard_map/slots_inside/pallas_call | solution.py:473
  109.8 3.7 %calm.1.calm_ref = f32[2,768,512]{2,1,0:T(8,128)} custom-call(f32[2,768,512]{2,1,0:T(8,128)} %own_ref.3, f32[3,4,768,128]{3,2,1,0:T(8,128)} %get-tuple-element.26.acc_ref), custom_call_target="tpu_custom_call" | custom-call | flops 1048576 | bytes 4194304 | tf_op jit(solution)/shard_map/calm/pallas_call | solution.py:499
  113.5 0.0 collective-permute-done.8.corner_ref
  113.5 0.0 copy-start.8
  113.5 0.0 collective-permute-done.7.below_ref
  113.5 0.0 collective-permute-done.6.right_ref
  113.5 13.7 %all-to-all-start = ((f32[128,12,128]{2,1,0:T(8,128)}), f32[128,12,128]{2,1,0:T(8,128)S(1)}, u32[]{:S(2)}, u32[]{:S(2)}) async-start(f32[128,12,128]{2,1,0:T(8,128)} %get-tuple-element.35), calls=%async_computation | async-start | bytes 2097152 | tf_op jit(solution)/shard_map/all_to_all | solution.py:579
  127.3 19.3 %all-to-all-done = f32[128,12,128]{2,1,0:T(8,128)S(1)} async-done(((f32[128,12,128]{2,1,0:T(8,128)}), f32[128,12,128]{2,1,0:T(8,128)S(1)}, u32[]{:S(2)}, u32[]{:S(2)}) %all-to-all-start) | async-done | bytes 786464 | tf_op jit(solution)/shard_map/all_to_all | solution.py:579
  146.5 0.1 reduce_sum.9
  146.7 0.0 copy-done.8
  146.7 0.1 divide_add_fusion
  146.8 0.9 broadcast_in_dim.8
  147.7 4.6 %all-to-all-start.1 = ((f32[128,8,128]{2,1,0:T(8,128)}), f32[128,8,128]{2,1,0:T(8,128)S(1)}, u32[]{:S(2)}, u32[]{:S(2)}) async-start(f32[128,8,128]{2,1,0:T(8,128)} %broadcast_in_dim.8), calls=%async_computation.1 | async-start | bytes 1048576 | tf_op jit(solution)/shard_map/all_to_all | solution.py:584
  152.3 7.3 %rim.1 = f32[2,768,512]{2,1,0:T(8,128)} custom-call(f32[2,768,512]{2,1,0:T(8,128)} %calm.1.calm_ref, f32[2,768,512]{2,1,0:T(8,128)} %own_ref.3, f32[3,4,768,128]{3,2,1,0:T(8,128)} %get-tuple-element.26.acc_ref, f32[4,768,128]{2,1,0:T(8,128)} %copy-done, f32[2,2,768,128]{3,2,1,0:T(8,128)} %collective-permute-done.6.right_ref, ...), custom_call_target="tpu_custom_call", output_to_operand_aliasing={{}: (0, {})} | custom-call | flops 1048576 | bytes 20971520 | tf_op jit(solution)/shard_map/rim/pallas_call | solution.py:520
  159.5 6.5 %all-to-all-done.1 = f32[128,8,128]{2,1,0:T(8,128)S(1)} async-done(((f32[128,8,128]{2,1,0:T(8,128)}), f32[128,8,128]{2,1,0:T(8,128)S(1)}, u32[]{:S(2)}, u32[]{:S(2)}) %all-to-all-start.1) | async-done | bytes 524320 | tf_op jit(solution)/shard_map/all_to_all | solution.py:584
  166.1 0.1 copy.11
  166.2 0.4 copy.12
  166.6 1.2 reshape.30
  (3 shorter events, 0.0 us)
Async XLA Ops:
  3.3 6.7 %copy-start.2 = (s32[1,1,2,24]{3,2,1,0:T(2,128)S(1)}, s32[1,1,2,24]{3,2,1,0:T(2,128)}, u32[]{:S(2)}) copy-start(s32[1,1,2,24]{3,2,1,0:T(2,128)} %param.10) | copy-start | bytes 580
  3.3 21.6 %copy-start.1 = (f32[2,256,256]{2,1,0:T(8,128)S(1)}, f32[2,256,256]{2,1,0:T(8,128)}, u32[]{:S(2)}) copy-start(f32[2,256,256]{2,1,0:T(8,128)} %refs_3_.5) | copy-start | bytes 1572868
  3.3 24.1 %collective-permute-start = (f32[2,768,256]{2,1,0:T(8,128)}, f32[2,768,256]{2,1,0:T(8,128)}, u32[]{:S(2)}, u32[]{:S(2)}) collective-permute-start(f32[2,768,256]{2,1,0:T(8,128)} %slice.25), channel_id=1, source_target_pairs={{1,0},{2,1},{3,2},{4,3},{5,4},{6,5},{7,6},{9,8},{10,9},{11,10},{12... | collective-permute-start | bytes 4718600 | tf_op jit(solution)/shard_map/ppermute | solution.py:433
  8.0 40.5 %collective-permute-start.4 = (f32[2,256,512]{2,1,0:T(8,128)S(1)}, f32[2,256,512]{2,1,0:T(8,128)S(1)}, u32[]{:S(2)}, u32[]{:S(2)}) collective-permute-start(f32[2,256,512]{2,1,0:T(8,128)S(1)} %slice.28), channel_id=1, source_target_pairs={{8,0},{9,1},{10,2},{11,3},{12,4},{13,5},{14,6},{15,7},{16,8},{17,9... | collective-permute-start | bytes 3145736 | tf_op jit(solution)/shard_map/ppermute | solution.py:433
  10.2 13.1 %collective-permute-start.1 = (s32[1,49]{1,0:T(1,128)S(1)}, s32[1,49]{1,0:T(1,128)S(1)}, u32[]{:S(2)}, u32[]{:S(2)}) collective-permute-start(s32[1,49]{1,0:T(1,128)S(1)} %pad_add_fusion.1), channel_id=1, source_target_pairs={{0,1},{1,2},{2,3},{3,4},{4,5},{5,6},{6,7},{8,9},{9,10},{10,11},{11... | collective-permute-start | bytes 596 | tf_op jit(solution)/shard_map/ppermute | solution.py:433
  13.7 10.9 %collective-permute-start.2 = (s32[1,49]{1,0:T(1,128)S(1)}, s32[1,49]{1,0:T(1,128)S(1)}, u32[]{:S(2)}, u32[]{:S(2)}) collective-permute-start(s32[1,49]{1,0:T(1,128)S(1)} %pad_add_fusion.1), channel_id=1, source_target_pairs={{0,8},{1,9},{2,10},{3,11},{4,12},{5,13},{6,14},{7,15},{8,16},{9,17... | collective-permute-start | bytes 596 | tf_op jit(solution)/shard_map/ppermute | solution.py:433
  18.0 6.6 %collective-permute-start.3 = (s32[1,49]{1,0:T(1,128)S(1)}, s32[1,49]{1,0:T(1,128)S(1)}, u32[]{:S(2)}, u32[]{:S(2)}) collective-permute-start(s32[1,49]{1,0:T(1,128)S(1)} %pad_add_fusion.1), channel_id=1, source_target_pairs={{0,9},{1,10},{2,11},{3,12},{4,13},{5,14},{6,15},{8,17},{9,18},{10,... | collective-permute-start | bytes 596 | tf_op jit(solution)/shard_map/ppermute | solution.py:433
  23.3 25.3 %collective-permute-start.5 = (f32[2,256,256]{2,1,0:T(8,128)}, f32[2,256,256]{2,1,0:T(8,128)S(1)}, u32[]{:S(2)}, u32[]{:S(2)}) collective-permute-start(f32[2,256,256]{2,1,0:T(8,128)} %slice.29), channel_id=1, source_target_pairs={{9,0},{10,1},{11,2},{12,3},{13,4},{14,5},{15,6},{17,8},{18,9},{19,... | collective-permute-start | bytes 1572872 | tf_op jit(solution)/shard_map/ppermute | solution.py:433
  24.7 2.7 %copy-start.3 = (bf16[4,256,768]{2,1,0:T(8,128)(2,1)S(1)}, bf16[4,256,768]{2,1,0:T(8,128)(2,1)}, u32[]{:S(2)}) copy-start(bf16[4,256,768]{2,1,0:T(8,128)(2,1)} %constant.34.clone.refs_4_) | copy-start | bytes 4718596
  26.3 1.1 copy-start
  27.4 1.4 copy-start.5
  47.4 1.1 copy-start.7
  48.5 40.5 %copy-start.4 = (bf16[4,256,768]{2,1,0:T(8,128)(2,1)S(1)}, bf16[4,256,768]{2,1,0:T(8,128)(2,1)}, u32[]{:S(2)}) copy-start(bf16[4,256,768]{2,1,0:T(8,128)(2,1)} %constant.34.clone.refs_4_) | copy-start | bytes 4718596
  48.5 40.5 %copy-start.6 = (bf16[4,768,256]{2,1,0:T(8,128)(2,1)S(1)}, bf16[4,768,256]{2,1,0:T(8,128)(2,1)}, u32[]{:S(2)}) copy-start(bf16[4,768,256]{2,1,0:T(8,128)(2,1)} %constant.35.clone.refs_5_) | copy-start | bytes 4718596
  71.3 42.3 %collective-permute-start.6 = (f32[2,2,768,128]{3,2,1,0:T(8,128)}, f32[2,2,768,128]{3,2,1,0:T(8,128)}, u32[]{:S(2)}, u32[]{:S(2)}) collective-permute-start(f32[2,2,768,128]{3,2,1,0:T(8,128)} %get-tuple-element.27), channel_id=1, source_target_pairs={{0,1},{1,2},{2,3},{3,4},{4,5},{5,6},{6,7},{8,9},{9,10},{10,11},{11... | collective-permute-start | bytes 4718600 | tf_op jit(solution)/shard_map/ppermute | solution.py:433
  73.2 40.3 %collective-permute-start.7 = (f32[2,4,256,128]{3,2,1,0:T(8,128)S(1)}, f32[2,4,256,128]{3,2,1,0:T(8,128)}, u32[]{:S(2)}, u32[]{:S(2)}) collective-permute-start(f32[2,4,256,128]{3,2,1,0:T(8,128)S(1)} %get-tuple-element.28), channel_id=1, source_target_pairs={{0,8},{1,9},{2,10},{3,11},{4,12},{5,13},{6,14},{7,15},{8,16},{9,17... | collective-permute-start | bytes 3145736 | tf_op jit(solution)/shard_map/ppermute | solution.py:433
  75.5 38.1 %collective-permute-start.8 = (f32[2,2,256,128]{3,2,1,0:T(8,128)}, f32[2,2,256,128]{3,2,1,0:T(8,128)S(1)}, u32[]{:S(2)}, u32[]{:S(2)}) collective-permute-start(f32[2,2,256,128]{3,2,1,0:T(8,128)} %get-tuple-element.29), channel_id=1, source_target_pairs={{0,9},{1,10},{2,11},{3,12},{4,13},{5,14},{6,15},{8,17},{9,18},{10,... | collective-permute-start | bytes 1572872 | tf_op jit(solution)/shard_map/ppermute | solution.py:433
  113.5 33.2 %copy-start.8 = (f32[2,2,256,128]{3,2,1,0:T(8,128)}, f32[2,2,256,128]{3,2,1,0:T(8,128)S(1)}, u32[]{:S(2)}) copy-start(f32[2,2,256,128]{3,2,1,0:T(8,128)S(1)} %collective-permute-done.8.corner_ref) | copy-start | bytes 1572868
  113.5 33.0 %all-to-all-start = ((f32[128,12,128]{2,1,0:T(8,128)}), f32[128,12,128]{2,1,0:T(8,128)S(1)}, u32[]{:S(2)}, u32[]{:S(2)}) async-start(f32[128,12,128]{2,1,0:T(8,128)} %get-tuple-element.35), calls=%async_computation | async-start | bytes 2097152 | tf_op jit(solution)/shard_map/all_to_all | solution.py:579
  147.7 18.4 %all-to-all-start.1 = ((f32[128,8,128]{2,1,0:T(8,128)}), f32[128,8,128]{2,1,0:T(8,128)S(1)}, u32[]{:S(2)}, u32[]{:S(2)}) async-start(f32[128,8,128]{2,1,0:T(8,128)} %broadcast_in_dim.8), calls=%async_computation.1 | async-start | bytes 1048576 | tf_op jit(solution)/shard_map/all_to_all | solution.py:584
